TPU v7x, 128 devices: a whole 4x4x4 slice. The times are simulated.
128 devices in a mesh: comp: 4 (over x), cell: 32 (over y, z, core).
Axes of the slice: x: 4, y: 4, z: 4, core: 2. Of those that a mesh axis runs over, the one named last changes fastest.
Arguments:
- biomass: float32 [48, 64, 16384], P(None, None, ('comp', 'cell')), may hold values from 0.1 to 2
- patch_area: float32 [48, 16384], P(None, ('comp', 'cell')), may hold values from 0.005 to 0.04
- cohort_traits: float32 [4, 64], replicated, may hold values from 0.1 to 1
- cell_forcing: float32 [5, 16384], P(None, ('comp', 'cell')), may hold values from 0.1 to 1
- disturb_weight: float32 [4, 16384], P(None, ('comp', 'cell')), may hold values from 0 to 0.25
- transitions: float32 [4, 48, 48], replicated, may hold values from 0 to 1
- land_source: int32 [131072], P(('comp', 'cell')), may hold values from -1 to 127, as said below
- pair_share: float32 [131072], P(('comp', 'cell')), may hold values from 0.05 to 0.35
- river_target: int32 [131072], P(('comp', 'cell')), may hold values from -1 to 2047, as said below
- downstream_step: int32 [262144], P(('comp', 'cell')), may hold values from 0 to 2047
- river_water: float32 [4, 262144], P(None, ('comp', 'cell')), may hold values from 0.5 to 2
- river_rates: float32 [4, 262144], P(None, ('comp', 'cell')), may hold values from 0.05 to 0.8
- capacity: float32 [262144], P(('comp', 'cell')), may hold values from 0.5 to 5
Outputs:
- new_biomass: float32 [48, 64, 16384], P(None, None, ('comp', 'cell'))
- flooded: float32 [16384], P(('comp', 'cell'))
- river_state: float32 [4, 262144], P(None, ('comp', 'cell'))
Inputs may be any that keep to these rules, and one draw needn't show every extreme that they name: `land_source`: A device's list has one block of 8 rows for each receiving device, in comp+cell order; live rows come first in every block, padding rows hold -1. Every device has at least one full block, and one receiving device gets full blocks from every device. `river_target`: row s of block i on device j is live exactly when row s of block j on device i of land_source is live, and then names the receiving river cell of device j; padding rows hold -1.
All inputs are finite; a program needn't handle non-finite values.
Results may differ from a plain program's by a relative error of at most 0.0001.
Values sent between devices are 32-bit elements; how exact they have to be, the bound alone decides.
A program may use at most 64 MiB of HBM per device.

v0:
```python
import jax
import jax.numpy as jnp
from jax import lax
from jax.sharding import PartitionSpec as P

NSUB = 12


highest = lax.Precision.HIGHEST


def in_blocks(value, dim, devices):
    before, after = (value.shape[:dim], value.shape[dim + 1 :])
    return jnp.moveaxis(value.reshape(*before, devices, -1, *after), dim, 0)


def in_order(blocks, dim):
    blocks = jnp.moveaxis(blocks, 0, dim)
    lengths = blocks.shape
    return blocks.reshape(*lengths[:dim], lengths[dim] * lengths[dim + 1], *lengths[dim + 2 :])


def joined_exchange(value, axis, axes, splits, concats):
    sizes = [lax.axis_size(a) for a in axes]
    blocks = in_blocks(value, splits[0], sizes[0])
    blocks = jnp.moveaxis(in_blocks(blocks, splits[1] + 1, sizes[1]), 0, 1)
    inside = blocks.shape[2:]
    blocks = blocks.reshape(-1, *inside)
    blocks = lax.all_to_all(blocks, axis, split_axis=0, concat_axis=0, tiled=True)
    blocks = in_order(blocks.reshape(*sizes, *inside), concats[0] + 1)
    return in_order(blocks, concats[1])


def from_behind(value, axis, steps):
    count = lax.axis_size(axis)
    initial, last = (max(0, -steps), min(count, count - steps))
    return lax.ppermute(value, axis, [(source, source + steps) for source in range(initial, last)])


def canopy(biomass, patch_area, cohort_traits, cell_forcing):
    leaf_area = biomass * cohort_traits[0][None, :, None]
    bin_count = biomass.shape[1]
    taller_mask = (jnp.arange(bin_count)[None, :] > jnp.arange(bin_count)[:, None]).astype(
        jnp.float32
    )
    leaf_above = jnp.einsum("kj,pjc->pkc", taller_mask, leaf_area, precision=highest)
    light_level = cell_forcing[0]
    assimilation = (
        cohort_traits[1][None, :, None]
        * leaf_area
        * jnp.exp(-0.05 * leaf_above)
        * (light_level / (light_level + 0.5))[None, None, :]
    )
    transpiration = 0.5 * jnp.sum(patch_area * jnp.sum(assimilation, axis=1), axis=0)
    wet_rain = cell_forcing[1] * cell_forcing[2]
    runoff = jnp.stack(
        [
            wet_rain * (1.0 - cell_forcing[4]),
            wet_rain * cell_forcing[4],
            cell_forcing[3] * jnp.exp(-0.5 * transpiration),
        ]
    )
    grown_mass = biomass * (1.0 - 0.1 * cohort_traits[2])[None, :, None] + 0.5 * assimilation
    return (grown_mass, runoff)


def transit(grown_mass, disturb_weight, transitions):
    patches, bin_count, cell_count = grown_mass.shape
    flat_mass = grown_mass.reshape(patches, bin_count * cell_count)
    transited = jnp.zeros_like(grown_mass)
    for kind_index in range(transitions.shape[0]):
        moved_mass = jnp.dot(
            transitions[kind_index],
            flat_mass,
            precision=highest,
            preferred_element_type=jnp.float32,
        )
        transited = (
            transited
            + moved_mass.reshape(patches, bin_count, cell_count)
            * disturb_weight[kind_index][None, None, :]
        )
    return transited


def scatter_pair(outflow, slots, segments):
    return jax.ops.segment_sum(outflow.T, slots, num_segments=segments).T


def shards(
    biomass,
    patch_area,
    cohort_traits,
    cell_forcing,
    disturb_weight,
    transitions,
    land_source,
    pair_share,
    river_target,
    downstream_step,
    river_water,
    river_rates,
    capacity,
):
    land_cells = biomass.shape[2]
    rivers = river_water.shape[1]
    comp_parts = lax.axis_size("comp")
    grown_mass, runoff = canopy(biomass, patch_area, cohort_traits, cell_forcing)
    is_live = land_source >= 0
    safe_source = jnp.where(is_live, land_source, 0)
    pair_values = jnp.where(
        is_live[None, :], pair_share[None, :] * jnp.take(runoff, safe_source, axis=1), 0.0
    )
    arrived = joined_exchange(
        pair_values.reshape(3, comp_parts, -1), ("comp", "cell"), ("comp", "cell"), (1, 2), (1, 2)
    ).reshape(3, -1)
    transited = transit(grown_mass, disturb_weight, transitions)
    has_target = river_target >= 0
    safe_target = jnp.where(has_target, river_target, rivers)
    runoff_in = jax.ops.segment_sum(arrived.T, safe_target, num_segments=rivers + 1)[:rivers].T
    local_cell = jnp.arange(rivers, dtype=jnp.int32)
    down_slot = jnp.where(downstream_step > 0, local_cell + downstream_step, 2 * rivers)
    fraction = 1.0 / NSUB
    surface_in = fraction * runoff_in[0:2]
    deep_in = jnp.stack([fraction * runoff_in[2], jnp.zeros_like(runoff_in[2])])
    hill_rate = river_rates[0:2]
    channel_rate = river_rates[2:4]

    def substep(sub_index, state_pair):
        hill_water, channel = state_pair
        hill_out = hill_rate * hill_water
        outflow = channel_rate * channel
        spread = scatter_pair(outflow, down_slot, 2 * rivers + 1)
        from_above = from_behind(spread[:, rivers : 2 * rivers], ("comp", "cell"), 1)
        inflow = spread[:, :rivers] + from_above
        return (hill_water - hill_out + surface_in, channel - outflow + hill_out + inflow + deep_in)

    hill_water, channel = lax.fori_loop(0, NSUB, substep, (river_water[0:2], river_water[2:4]))
    stored_total = channel[0] + channel[1]
    inundation = stored_total / (stored_total + capacity)
    flood_back = jnp.where(has_target, inundation[jnp.where(has_target, river_target, 0)], 0.0)
    returned = lax.all_to_all(
        lax.all_to_all(
            flood_back.reshape(comp_parts, -1), "cell", split_axis=1, concat_axis=1, tiled=True
        ),
        "comp",
        split_axis=0,
        concat_axis=0,
        tiled=True,
    ).reshape(-1)
    flooded = jax.ops.segment_sum(
        pair_share * returned,
        jnp.where(is_live, land_source, land_cells),
        num_segments=land_cells + 1,
    )[:land_cells]
    new_biomass = transited * jnp.exp(-cohort_traits[3][None, :, None] * flooded[None, None, :])
    river_state = jnp.concatenate([hill_water, channel], axis=0)
    return (new_biomass, flooded, river_state)


def solution(mesh):
    return jax.shard_map(
        shards,
        mesh=mesh,
        in_specs=(
            P(None, None, ("comp", "cell")),
            P(None, ("comp", "cell")),
            P(),
            P(None, ("comp", "cell")),
            P(None, ("comp", "cell")),
            P(),
            P(("comp", "cell")),
            P(("comp", "cell")),
            P(("comp", "cell")),
            P(("comp", "cell")),
            P(None, ("comp", "cell")),
            P(None, ("comp", "cell")),
            P(("comp", "cell")),
        ),
        out_specs=(P(None, None, ("comp", "cell")), P(("comp", "cell")), P(None, ("comp", "cell"))),
        check_vma=False,
    )
```

profile of v0, /device:TPU:1, one launch (start us, length us, event | category | flops | bytes accessed | tf_op | source)
XLA Modules:
  0.0 398.4 jit_solution(263364392975987532)
XLA Ops:
  12.3 11.5 %all-to-all-start = ((f32[128,3,1,8]{3,2,1,0:T(1,128)}), f32[128,3,1,8]{3,2,1,0:T(1,128)S(1)}, u32[]{:S(2)}, u32[]{:S(2)}) async-start(f32[128,3,1,8]{3,2,1,0:T(1,128)} %bitcast.27), calls=%async_computation | async-start | bytes 393216 | tf_op jit(solution)/shard_map/all_to_all | solution.py:29
  23.9 3.7 fusion.18
  27.5 3.6 fusion.21
  31.3 3.7 fusion.24
  40.1 6.5 %scatter_custom_fusion.1 = f32[2049,3]{1,0:T(8,128)S(1)} fusion(s32[1024]{0:T(1024)S(1)} %get-tuple-element.76, f32[1024,3]{1,0:T(8,128)S(1)} %copy.88, f32[]{:T(128)} %constant.23.clone.1), kind=kCustom, calls=%fused_computation.45 | custom fusion | flops 3072 | bytes 24592 | tf_op jit(solution)/shard_map/scatter-add | solution.py:120
  49.2 300.4 %while.12 = (s32[]{:T(128)}, f32[2,2048]{0,1:T(8,128)}, f32[2,2048]{0,1:T(8,128)S(1)}, f32[2,2048]{0,1:T(8,128)}, f32[2,2048]{0,1:T(8,128)}, /*index=5*/f32[2,20...) while((s32[]{:T(128)}, f32[2,2048]{0,1:T(8,128)}, f32[2,2048]{0,1:T(8,128)S(1)}, ...), condition=%wide.region_5.6_spmd, body=%wide.region_3.5_spmd.sunk | while | flops 45058 | bytes 1851629 | solution.py:138
  49.2 12.4 %scatter_custom_fusion.9 = f32[4097,2]{1,0:T(8,128)S(1)} fusion(s32[2048]{0:T(1024)S(1)} %get-tuple-element.177, f32[]{:T(128)} %constant.23.clone.1..sunk, f32[2,2048]{0,1:T(8,128)} %get-tuple-element.176, f32[2,2048]{0,1:T(8,128)S(1)} %get-tuple-element.163), kind=kCustom, calls=%fused_computation.5.clone.1 | custom fusion | flops 8192 | bytes 1097740 | tf_op jit(solution)/shard_map/while/body/eval_jaxpr/scatter-add | solution.py:87
  64.7 3.7 collective-permute-start
  75.2 12.4 %scatter_custom_fusion.9 = f32[4097,2]{1,0:T(8,128)S(1)} fusion(s32[2048]{0:T(1024)S(1)} %get-tuple-element.177, f32[]{:T(128)} %constant.23.clone.1..sunk, f32[2,2048]{0,1:T(8,128)} %get-tuple-element.176, f32[2,2048]{0,1:T(8,128)S(1)} %get-tuple-element.163), kind=kCustom, calls=%fused_computation.5.clone.1 | custom fusion | flops 8192 | bytes 1097740 | tf_op jit(solution)/shard_map/while/body/eval_jaxpr/scatter-add | solution.py:87
  99.5 12.4 %scatter_custom_fusion.9 = f32[4097,2]{1,0:T(8,128)S(1)} fusion(s32[2048]{0:T(1024)S(1)} %get-tuple-element.177, f32[]{:T(128)} %constant.23.clone.1..sunk, f32[2,2048]{0,1:T(8,128)} %get-tuple-element.176, f32[2,2048]{0,1:T(8,128)S(1)} %get-tuple-element.163), kind=kCustom, calls=%fused_computation.5.clone.1 | custom fusion | flops 8192 | bytes 1097740 | tf_op jit(solution)/shard_map/while/body/eval_jaxpr/scatter-add | solution.py:87
  125.4 12.4 %scatter_custom_fusion.9 = f32[4097,2]{1,0:T(8,128)S(1)} fusion(s32[2048]{0:T(1024)S(1)} %get-tuple-element.177, f32[]{:T(128)} %constant.23.clone.1..sunk, f32[2,2048]{0,1:T(8,128)} %get-tuple-element.176, f32[2,2048]{0,1:T(8,128)S(1)} %get-tuple-element.163), kind=kCustom, calls=%fused_computation.5.clone.1 | custom fusion | flops 8192 | bytes 1097740 | tf_op jit(solution)/shard_map/while/body/eval_jaxpr/scatter-add | solution.py:87
  149.8 12.4 %scatter_custom_fusion.9 = f32[4097,2]{1,0:T(8,128)S(1)} fusion(s32[2048]{0:T(1024)S(1)} %get-tuple-element.177, f32[]{:T(128)} %constant.23.clone.1..sunk, f32[2,2048]{0,1:T(8,128)} %get-tuple-element.176, f32[2,2048]{0,1:T(8,128)S(1)} %get-tuple-element.163), kind=kCustom, calls=%fused_computation.5.clone.1 | custom fusion | flops 8192 | bytes 1097740 | tf_op jit(solution)/shard_map/while/body/eval_jaxpr/scatter-add | solution.py:87
  175.4 12.4 %scatter_custom_fusion.9 = f32[4097,2]{1,0:T(8,128)S(1)} fusion(s32[2048]{0:T(1024)S(1)} %get-tuple-element.177, f32[]{:T(128)} %constant.23.clone.1..sunk, f32[2,2048]{0,1:T(8,128)} %get-tuple-element.176, f32[2,2048]{0,1:T(8,128)S(1)} %get-tuple-element.163), kind=kCustom, calls=%fused_computation.5.clone.1 | custom fusion | flops 8192 | bytes 1097740 | tf_op jit(solution)/shard_map/while/body/eval_jaxpr/scatter-add | solution.py:87
  199.8 12.4 %scatter_custom_fusion.9 = f32[4097,2]{1,0:T(8,128)S(1)} fusion(s32[2048]{0:T(1024)S(1)} %get-tuple-element.177, f32[]{:T(128)} %constant.23.clone.1..sunk, f32[2,2048]{0,1:T(8,128)} %get-tuple-element.176, f32[2,2048]{0,1:T(8,128)S(1)} %get-tuple-element.163), kind=kCustom, calls=%fused_computation.5.clone.1 | custom fusion | flops 8192 | bytes 1097740 | tf_op jit(solution)/shard_map/while/body/eval_jaxpr/scatter-add | solution.py:87
  224.8 12.4 %scatter_custom_fusion.9 = f32[4097,2]{1,0:T(8,128)S(1)} fusion(s32[2048]{0:T(1024)S(1)} %get-tuple-element.177, f32[]{:T(128)} %constant.23.clone.1..sunk, f32[2,2048]{0,1:T(8,128)} %get-tuple-element.176, f32[2,2048]{0,1:T(8,128)S(1)} %get-tuple-element.163), kind=kCustom, calls=%fused_computation.5.clone.1 | custom fusion | flops 8192 | bytes 1097740 | tf_op jit(solution)/shard_map/while/body/eval_jaxpr/scatter-add | solution.py:87
  249.1 12.4 %scatter_custom_fusion.9 = f32[4097,2]{1,0:T(8,128)S(1)} fusion(s32[2048]{0:T(1024)S(1)} %get-tuple-element.177, f32[]{:T(128)} %constant.23.clone.1..sunk, f32[2,2048]{0,1:T(8,128)} %get-tuple-element.176, f32[2,2048]{0,1:T(8,128)S(1)} %get-tuple-element.163), kind=kCustom, calls=%fused_computation.5.clone.1 | custom fusion | flops 8192 | bytes 1097740 | tf_op jit(solution)/shard_map/while/body/eval_jaxpr/scatter-add | solution.py:87
  274.9 12.4 %scatter_custom_fusion.9 = f32[4097,2]{1,0:T(8,128)S(1)} fusion(s32[2048]{0:T(1024)S(1)} %get-tuple-element.177, f32[]{:T(128)} %constant.23.clone.1..sunk, f32[2,2048]{0,1:T(8,128)} %get-tuple-element.176, f32[2,2048]{0,1:T(8,128)S(1)} %get-tuple-element.163), kind=kCustom, calls=%fused_computation.5.clone.1 | custom fusion | flops 8192 | bytes 1097740 | tf_op jit(solution)/shard_map/while/body/eval_jaxpr/scatter-add | solution.py:87
  299.3 12.4 %scatter_custom_fusion.9 = f32[4097,2]{1,0:T(8,128)S(1)} fusion(s32[2048]{0:T(1024)S(1)} %get-tuple-element.177, f32[]{:T(128)} %constant.23.clone.1..sunk, f32[2,2048]{0,1:T(8,128)} %get-tuple-element.176, f32[2,2048]{0,1:T(8,128)S(1)} %get-tuple-element.163), kind=kCustom, calls=%fused_computation.5.clone.1 | custom fusion | flops 8192 | bytes 1097740 | tf_op jit(solution)/shard_map/while/body/eval_jaxpr/scatter-add | solution.py:87
  325.2 12.4 %scatter_custom_fusion.9 = f32[4097,2]{1,0:T(8,128)S(1)} fusion(s32[2048]{0:T(1024)S(1)} %get-tuple-element.177, f32[]{:T(128)} %constant.23.clone.1..sunk, f32[2,2048]{0,1:T(8,128)} %get-tuple-element.176, f32[2,2048]{0,1:T(8,128)S(1)} %get-tuple-element.163), kind=kCustom, calls=%fused_computation.5.clone.1 | custom fusion | flops 8192 | bytes 1097740 | tf_op jit(solution)/shard_map/while/body/eval_jaxpr/scatter-add | solution.py:87
  350.3 6.2 %gather_fusion.1 = f32[1024]{0:T(1024)S(1)} fusion(f32[2048]{0:T(1024)S(1)} %add_divide_fusion, s32[1024]{0:T(1024)S(1)} %get-tuple-element.75), kind=kCustom, calls=%fused_computation.1 | custom fusion | bytes 12288 | tf_op jit(solution)/shard_map/gather | solution.py:141
  357.2 10.2 %all-to-all-start.1 = ((f32[4,32,8]{2,0,1:T(4,128)}), f32[4,32,8]{2,0,1:T(4,128)S(1)}, u32[]{:S(2)}, u32[]{:S(2)}) async-start(f32[4,32,8]{2,0,1:T(4,128)} %copy.90), calls=%async_computation.1 | async-start | bytes 131072 | tf_op jit(solution)/shard_map/all_to_all | solution.py:143
  378.0 3.7 all-to-all-start.2
  385.8 7.6 %scatter_custom_fusion.2 = f32[129]{0:T(256)S(1)} fusion(s32[1024]{0:T(1024)S(1)} %get-tuple-element.80, f32[1024]{0:T(1024)S(1)} %mul.247, f32[]{:T(128)} %constant.23.clone.1), kind=kCustom, calls=%fused_computation.78 | custom fusion | flops 1024 | bytes 520 | tf_op jit(solution)/shard_map/scatter-add | solution.py:151
  393.5 4.9 %fusion.5 = f32[48,64,128]{2,1,0:T(8,128)} fusion(f32[6,8,64,128]{3,2,1,0:T(8,128)} %copy.104, f32[6,8,64,128]{3,2,1,0:T(8,128)} %copy.103, f32[6,8,64,128]{3,2,1,0:T(8,128)} %copy.102, f32[6,8,64,128]{3,2,1,0:T(8,128)} %copy.101, f32[64,128]{1,0:T(8,128)S(1)} %multiply_exponential_fusion, f32[128]{0:T(128)S(1)} %get-tuple-element.86, ...), kind=kLoop, calls=%fused_computation.14 | loop fusion | flops 3145728 | bytes 7899136 | tf_op jit(solution)/shard_map/mul | solution.py:156
  (291 shorter events, 182.5 us)
Async XLA Ops:
  7.2 24.1 %copy-start.4 = (f32[48,64,128]{2,1,0:T(8,128)}, f32[48,64,128]{2,1,0:T(8,128)S(1)}, u32[]{:S(2)}) copy-start(f32[48,64,128]{2,1,0:T(8,128)S(1)} %get-tuple-element.70) | copy-start | bytes 4718596
  7.2 16.7 %copy-start.9 = (f32[4,48,48]{2,1,0:T(8,128)S(1)}, f32[4,48,48]{2,1,0:T(8,128)}, u32[]{:S(2)}) copy-start(f32[4,48,48]{2,1,0:T(8,128)} %param.20) | copy-start | bytes 110596
  12.3 27.1 %all-to-all-start = ((f32[128,3,1,8]{3,2,1,0:T(1,128)}), f32[128,3,1,8]{3,2,1,0:T(1,128)S(1)}, u32[]{:S(2)}, u32[]{:S(2)}) async-start(f32[128,3,1,8]{3,2,1,0:T(1,128)} %bitcast.27), calls=%async_computation | async-start | bytes 393216 | tf_op jit(solution)/shard_map/all_to_all | solution.py:29
  63.1 5.3 %copy-start = (f32[2,2048]{0,1:T(8,128)S(1)}, f32[2,2048]{0,1:T(8,128)}, u32[]{:S(2)}) copy-start(f32[2,2048]{0,1:T(8,128)} %get-tuple-element.176) | copy-start | bytes 49156 | tf_op jit(solution)/shard_map/while
  64.7 9.5 %collective-permute-start = (f32[2,2048]{1,0:T(2,128)S(1)}, f32[2,2048]{1,0:T(2,128)S(1)}, u32[]{:S(2)}, u32[]{:S(2)}) collective-permute-start(f32[2,2048]{1,0:T(2,128)S(1)} %copy.127), channel_id=1, source_target_pairs={{0,1},{1,2},{2,3},{3,4},{4,5},{5,6},{6,7},{7,8},{8,9},{9,10},{10,1... | collective-permute-start | bytes 49160 | tf_op jit(solution)/shard_map/while/body/eval_jaxpr/ppermute | solution.py:37
  90.7 7.8 %collective-permute-start = (f32[2,2048]{1,0:T(2,128)S(1)}, f32[2,2048]{1,0:T(2,128)S(1)}, u32[]{:S(2)}, u32[]{:S(2)}) collective-permute-start(f32[2,2048]{1,0:T(2,128)S(1)} %copy.127), channel_id=1, source_target_pairs={{0,1},{1,2},{2,3},{3,4},{4,5},{5,6},{6,7},{7,8},{8,9},{9,10},{10,1... | collective-permute-start | bytes 49160 | tf_op jit(solution)/shard_map/while/body/eval_jaxpr/ppermute | solution.py:37
  113.4 5.3 %copy-start = (f32[2,2048]{0,1:T(8,128)S(1)}, f32[2,2048]{0,1:T(8,128)}, u32[]{:S(2)}) copy-start(f32[2,2048]{0,1:T(8,128)} %get-tuple-element.176) | copy-start | bytes 49156 | tf_op jit(solution)/shard_map/while
  115.0 9.4 %collective-permute-start = (f32[2,2048]{1,0:T(2,128)S(1)}, f32[2,2048]{1,0:T(2,128)S(1)}, u32[]{:S(2)}, u32[]{:S(2)}) collective-permute-start(f32[2,2048]{1,0:T(2,128)S(1)} %copy.127), channel_id=1, source_target_pairs={{0,1},{1,2},{2,3},{3,4},{4,5},{5,6},{6,7},{7,8},{8,9},{9,10},{10,1... | collective-permute-start | bytes 49160 | tf_op jit(solution)/shard_map/while/body/eval_jaxpr/ppermute | solution.py:37
  140.9 7.8 %collective-permute-start = (f32[2,2048]{1,0:T(2,128)S(1)}, f32[2,2048]{1,0:T(2,128)S(1)}, u32[]{:S(2)}, u32[]{:S(2)}) collective-permute-start(f32[2,2048]{1,0:T(2,128)S(1)} %copy.127), channel_id=1, source_target_pairs={{0,1},{1,2},{2,3},{3,4},{4,5},{5,6},{6,7},{7,8},{8,9},{9,10},{10,1... | collective-permute-start | bytes 49160 | tf_op jit(solution)/shard_map/while/body/eval_jaxpr/ppermute | solution.py:37
  163.7 5.0 %copy-start = (f32[2,2048]{0,1:T(8,128)S(1)}, f32[2,2048]{0,1:T(8,128)}, u32[]{:S(2)}) copy-start(f32[2,2048]{0,1:T(8,128)} %get-tuple-element.176) | copy-start | bytes 49156 | tf_op jit(solution)/shard_map/while
  165.3 9.1 %collective-permute-start = (f32[2,2048]{1,0:T(2,128)S(1)}, f32[2,2048]{1,0:T(2,128)S(1)}, u32[]{:S(2)}, u32[]{:S(2)}) collective-permute-start(f32[2,2048]{1,0:T(2,128)S(1)} %copy.127), channel_id=1, source_target_pairs={{0,1},{1,2},{2,3},{3,4},{4,5},{5,6},{6,7},{7,8},{8,9},{9,10},{10,1... | collective-permute-start | bytes 49160 | tf_op jit(solution)/shard_map/while/body/eval_jaxpr/ppermute | solution.py:37
  190.9 7.9 %collective-permute-start = (f32[2,2048]{1,0:T(2,128)S(1)}, f32[2,2048]{1,0:T(2,128)S(1)}, u32[]{:S(2)}, u32[]{:S(2)}) collective-permute-start(f32[2,2048]{1,0:T(2,128)S(1)} %copy.127), channel_id=1, source_target_pairs={{0,1},{1,2},{2,3},{3,4},{4,5},{5,6},{6,7},{7,8},{8,9},{9,10},{10,1... | collective-permute-start | bytes 49160 | tf_op jit(solution)/shard_map/while/body/eval_jaxpr/ppermute | solution.py:37
  215.3 8.5 %collective-permute-start = (f32[2,2048]{1,0:T(2,128)S(1)}, f32[2,2048]{1,0:T(2,128)S(1)}, u32[]{:S(2)}, u32[]{:S(2)}) collective-permute-start(f32[2,2048]{1,0:T(2,128)S(1)} %copy.127), channel_id=1, source_target_pairs={{0,1},{1,2},{2,3},{3,4},{4,5},{5,6},{6,7},{7,8},{8,9},{9,10},{10,1... | collective-permute-start | bytes 49160 | tf_op jit(solution)/shard_map/while/body/eval_jaxpr/ppermute | solution.py:37
  240.3 7.8 %collective-permute-start = (f32[2,2048]{1,0:T(2,128)S(1)}, f32[2,2048]{1,0:T(2,128)S(1)}, u32[]{:S(2)}, u32[]{:S(2)}) collective-permute-start(f32[2,2048]{1,0:T(2,128)S(1)} %copy.127), channel_id=1, source_target_pairs={{0,1},{1,2},{2,3},{3,4},{4,5},{5,6},{6,7},{7,8},{8,9},{9,10},{10,1... | collective-permute-start | bytes 49160 | tf_op jit(solution)/shard_map/while/body/eval_jaxpr/ppermute | solution.py:37
  263.0 5.2 %copy-start = (f32[2,2048]{0,1:T(8,128)S(1)}, f32[2,2048]{0,1:T(8,128)}, u32[]{:S(2)}) copy-start(f32[2,2048]{0,1:T(8,128)} %get-tuple-element.176) | copy-start | bytes 49156 | tf_op jit(solution)/shard_map/while
  264.6 9.3 %collective-permute-start = (f32[2,2048]{1,0:T(2,128)S(1)}, f32[2,2048]{1,0:T(2,128)S(1)}, u32[]{:S(2)}, u32[]{:S(2)}) collective-permute-start(f32[2,2048]{1,0:T(2,128)S(1)} %copy.127), channel_id=1, source_target_pairs={{0,1},{1,2},{2,3},{3,4},{4,5},{5,6},{6,7},{7,8},{8,9},{9,10},{10,1... | collective-permute-start | bytes 49160 | tf_op jit(solution)/shard_map/while/body/eval_jaxpr/ppermute | solution.py:37
  290.4 7.8 %collective-permute-start = (f32[2,2048]{1,0:T(2,128)S(1)}, f32[2,2048]{1,0:T(2,128)S(1)}, u32[]{:S(2)}, u32[]{:S(2)}) collective-permute-start(f32[2,2048]{1,0:T(2,128)S(1)} %copy.127), channel_id=1, source_target_pairs={{0,1},{1,2},{2,3},{3,4},{4,5},{5,6},{6,7},{7,8},{8,9},{9,10},{10,1... | collective-permute-start | bytes 49160 | tf_op jit(solution)/shard_map/while/body/eval_jaxpr/ppermute | solution.py:37
  313.2 5.3 %copy-start = (f32[2,2048]{0,1:T(8,128)S(1)}, f32[2,2048]{0,1:T(8,128)}, u32[]{:S(2)}) copy-start(f32[2,2048]{0,1:T(8,128)} %get-tuple-element.176) | copy-start | bytes 49156 | tf_op jit(solution)/shard_map/while
  314.8 9.4 %collective-permute-start = (f32[2,2048]{1,0:T(2,128)S(1)}, f32[2,2048]{1,0:T(2,128)S(1)}, u32[]{:S(2)}, u32[]{:S(2)}) collective-permute-start(f32[2,2048]{1,0:T(2,128)S(1)} %copy.127), channel_id=1, source_target_pairs={{0,1},{1,2},{2,3},{3,4},{4,5},{5,6},{6,7},{7,8},{8,9},{9,10},{10,1... | collective-permute-start | bytes 49160 | tf_op jit(solution)/shard_map/while/body/eval_jaxpr/ppermute | solution.py:37
  340.7 7.8 %collective-permute-start = (f32[2,2048]{1,0:T(2,128)S(1)}, f32[2,2048]{1,0:T(2,128)S(1)}, u32[]{:S(2)}, u32[]{:S(2)}) collective-permute-start(f32[2,2048]{1,0:T(2,128)S(1)} %copy.127), channel_id=1, source_target_pairs={{0,1},{1,2},{2,3},{3,4},{4,5},{5,6},{6,7},{7,8},{8,9},{9,10},{10,1... | collective-permute-start | bytes 49160 | tf_op jit(solution)/shard_map/while/body/eval_jaxpr/ppermute | solution.py:37
  350.3 17.2 %copy-start.5 = (f32[48,64,128]{2,1,0:T(8,128)S(1)}, f32[48,64,128]{2,1,0:T(8,128)}, u32[]{:S(2)}) copy-start(f32[48,64,128]{2,1,0:T(8,128)} %copy-done.4) | copy-start | bytes 4718596
  357.2 20.1 %all-to-all-start.1 = ((f32[4,32,8]{2,0,1:T(4,128)}), f32[4,32,8]{2,0,1:T(4,128)S(1)}, u32[]{:S(2)}, u32[]{:S(2)}) async-start(f32[4,32,8]{2,0,1:T(4,128)} %copy.90), calls=%async_computation.1 | async-start | bytes 131072 | tf_op jit(solution)/shard_map/all_to_all | solution.py:143
  378.0 7.8 %all-to-all-start.2 = ((f32[4,1,256]{2,1,0:T(1,128)}), f32[4,1,256]{2,1,0:T(1,128)S(1)}, u32[]{:S(2)}, u32[]{:S(2)}) async-start(f32[4,1,256]{2,1,0:T(1,128)} %all_to_all.20), calls=%async_computation.2 | async-start | bytes 8192 | tf_op jit(solution)/shard_map/all_to_all | solution.py:142
  393.4 5.0 %copy-start.19 = (f32[128]{0:T(128)}, f32[128]{0:T(128)S(1)}, u32[]{:S(2)}) copy-start(f32[128]{0:T(128)S(1)} %slice.114) | copy-start | bytes 1540
  (44 other events, 103.7 us)
where the time goes:
time: 401 us; the launch traced here: 398 us
  other arithmetic  217 us (54%)
  local copies, waits for them, and re-layouts  101 us (25%)
  starting transfers between devices  58.1 us (14%)
  matrix products  17.1 us (4%)
    scatter-add x12, other arithmetic, scatter_pair(): return jax.ops.segment_sum(outflow.T, slots, num_segments=segments).T  149 us
    add x12, other arithmetic, substep(): hill_water - hill_out + surface_in  41.2 us
    slice x24, local copies, waits for them, and re-layouts, substep(): from_above = from_behind(spread[:, rivers:2 * rivers], ('comp', 'cell'), 1)  36.8 us
    ppermute x12, starting transfers between devices, from_behind(): lax.ppermute(value, axis, [(source, source + steps) for source in range(i...  32.8 us
    sub x12, local copies, waits for them, and re-layouts, substep(): channel - outflow + hill_out + inflow + deep_in  19.7 us
    dot_general x4, matrix products, transit(): jnp.dot(transitions[kind_index], flat_mass, precision=highest, preferred_...  13.5 us
    all_to_all x1, starting transfers between devices, joined_exchange(): lax.all_to_all(blocks, axis, split_axis=0, concat_axis=0, tiled=True)  11.5 us
    unnamed x42, local copies, waits for them, and re-layouts  11.2 us
  transfers between devices with their start and end apart: 15, of which 1 were waited for; matrix products, arithmetic and copies ran while one was open for 24% of the time, Pallas kernels for 0%

commit v1 on v0

v1 whole, which is shorter than its diff:
```python
import jax
import jax.numpy as jnp
from jax import lax
from jax.experimental import pallas as pl
from jax.experimental.pallas import tpu as pltpu
from jax.sharding import PartitionSpec as P

MESH = pl.DeviceIdType.MESH
F32 = jnp.float32
BF16 = jnp.bfloat16

NSUB = 12
PATCH = 48
BINS = 64
KINDS = 4
LANES = 128
NA = 16
NB = 8
ROWS = 16
CHUNK = 4


def split2(x):
    hi = x.astype(BF16).astype(F32)
    return hi, x - hi


def split3(x):
    hi, rest = split2(x)
    mid, low = split2(rest)
    return hi, mid, low


def nt_dot(a, b):
    return lax.dot_general(a, b, (((1,), (1,)), ((), ())), preferred_element_type=F32)


def nn_dot(a, b):
    return jnp.dot(a, b, preferred_element_type=F32)


def main_kernel(
    bio, area, traits, forcing, weight, trans, src, share, tgt, step, water, rates, cap,
    tr_out, flood_out, river_out,
    grown, tmat, rhs, onehot_src, lane_rcv, row_rcv, lane_step, row_step, lhs_step, lhs_rcv, lhs_back, state,
    send_a, recv_a, send_b, recv_b, send_rb, recv_rb, send_ra, recv_ra, send_ring, recv_ring,
    sa_s, sa_r, sb_s, sb_r, rb_s, rb_r, ra_s, ra_r, ring_s, ring_r,
):
    my_x = lax.axis_index("comp")
    cell = lax.axis_index("cell")
    my_y, my_b = cell // NB, cell % NB
    my_a = my_x * 4 + my_y
    me = my_x * 32 + cell
    nxt = (me + 1) % 128
    prv = (me + 127) % 128

    def peer_a(other):
        return (other // 4, (other % 4) * NB + my_b)

    def peer_b(other):
        return (my_x, my_y * NB + other)

    barrier = pltpu.get_barrier_semaphore()

    def greet_a(k, _):
        pl.semaphore_signal(barrier, inc=1, device_id=peer_a((my_a + k) % NA), device_id_type=MESH)
        return 0

    def greet_b(k, _):
        pl.semaphore_signal(barrier, inc=1, device_id=peer_b((my_b + k) % NB), device_id_type=MESH)
        return 0

    lax.fori_loop(1, NA, greet_a, 0)
    lax.fori_loop(1, NB, greet_b, 0)
    for other in (nxt, prv):
        pl.semaphore_signal(barrier, inc=1, device_id=(other // 32, other % 32), device_id_type=MESH)

    sub8 = lax.broadcasted_iota(jnp.int32, (8, LANES), 0)
    lane8 = lax.broadcasted_iota(jnp.int32, (8, LANES), 1)
    block8 = lane8 >> 3
    sub16 = lax.broadcasted_iota(jnp.int32, (16, LANES), 0)
    sub128 = lax.broadcasted_iota(jnp.int32, (LANES, LANES), 0)

    for r in range(8):
        hot = jnp.where(sub128 == src[r : r + 1, :], 1.0, 0.0)
        onehot_src[:, r * LANES : (r + 1) * LANES] = hot.astype(BF16)

    light = forcing[0:1, :]
    light_factor = light / (light + 0.5)

    def canopy_bin(i, carry):
        above, total = carry
        k = BINS - 1 - i
        mass = bio[pl.ds(k, PATCH, stride=BINS), :]
        leaf = mass * traits[0, k]
        gain = (traits[1, k] * light_factor) * leaf * jnp.exp(-0.05 * above)
        grown[pl.ds(pl.multiple_of(k * PATCH, PATCH), PATCH), :] = mass * (1.0 - 0.1 * traits[2, k]) + 0.5 * gain
        return above + leaf, total + gain

    zero48 = jnp.zeros((PATCH, LANES), F32)
    _, total = lax.fori_loop(0, BINS, canopy_bin, (zero48, zero48), unroll=4)
    transpiration = 0.5 * jnp.sum(area[...] * total, axis=0, keepdims=True)
    wet = forcing[1:2, :] * forcing[2:3, :]
    frozen = forcing[4:5, :]
    row0 = wet * (1.0 - frozen)
    row1 = wet * frozen
    row2 = forcing[3:4, :] * jnp.exp(-0.5 * transpiration)
    runoff = jnp.where(sub8 == 0, row0, jnp.where(sub8 == 1, row1, jnp.where(sub8 == 2, row2, 0.0)))
    parts = split3(runoff)
    lhs = jnp.concatenate([*parts, jnp.zeros((8, LANES), F32)], axis=0).astype(BF16)
    picked = nn_dot(lhs, onehot_src[...])
    picked = picked[0:8] + picked[8:16] + picked[16:24]
    for r in range(8):
        send_a[r] = picked[:, r * LANES : (r + 1) * LANES] * share[r : r + 1, :]

    def copy_a(k):
        other = (my_a + k) % NA
        return pltpu.make_async_remote_copy(
            src_ref=send_a.at[other // 2], dst_ref=recv_a.at[my_a], send_sem=sa_s.at[k], recv_sem=sa_r.at[my_a],
            device_id=peer_a(other), device_id_type=MESH)

    def arrive_a(k):
        other = (my_a + k) % NA
        return pltpu.make_async_remote_copy(
            src_ref=send_a.at[0], dst_ref=recv_a.at[other], send_sem=sa_s.at[k], recv_sem=sa_r.at[other],
            device_id=peer_a(other), device_id_type=MESH)

    def copy_b(k):
        other = (my_b + k) % NB
        return pltpu.make_async_remote_copy(
            src_ref=send_b.at[other], dst_ref=recv_b.at[my_b], send_sem=sb_s.at[k], recv_sem=sb_r.at[my_b],
            device_id=peer_b(other), device_id_type=MESH)

    def arrive_b(k):
        other = (my_b + k) % NB
        return pltpu.make_async_remote_copy(
            src_ref=send_b.at[other], dst_ref=recv_b.at[other], send_sem=sb_s.at[k], recv_sem=sb_r.at[other],
            device_id=peer_b(other), device_id_type=MESH)

    def copy_rb(k):
        other = (my_b + k) % NB
        return pltpu.make_async_remote_copy(
            src_ref=send_rb.at[other], dst_ref=recv_rb.at[my_b], send_sem=rb_s.at[k], recv_sem=rb_r.at[my_b],
            device_id=peer_b(other), device_id_type=MESH)

    def arrive_rb(k):
        other = (my_b + k) % NB
        return pltpu.make_async_remote_copy(
            src_ref=send_rb.at[other], dst_ref=recv_rb.at[other], send_sem=rb_s.at[k], recv_sem=rb_r.at[other],
            device_id=peer_b(other), device_id_type=MESH)

    def copy_ra(k):
        other = (my_a + k) % NA
        return pltpu.make_async_remote_copy(
            src_ref=send_ra, dst_ref=recv_ra.at[my_a], send_sem=ra_s.at[k], recv_sem=ra_r.at[my_a],
            device_id=peer_a(other), device_id_type=MESH)

    def arrive_ra(k):
        other = (my_a + k) % NA
        return pltpu.make_async_remote_copy(
            src_ref=send_ra, dst_ref=recv_ra.at[other], send_sem=ra_s.at[k], recv_sem=ra_r.at[other],
            device_id=peer_a(other), device_id_type=MESH)

    def ring(t):
        return pltpu.make_async_remote_copy(
            src_ref=send_ring.at[t], dst_ref=recv_ring.at[t], send_sem=ring_s.at[t], recv_sem=ring_r.at[t],
            device_id=(nxt // 32, nxt % 32), device_id_type=MESH)

    def each(count, action):
        def one(k, _):
            action(k)
            return 0

        lax.fori_loop(1, count, one, 0)

    pl.semaphore_wait(barrier, NA + NB)
    each(NA, lambda k: copy_a(k).start())
    recv_a[my_a] = send_a[my_a // 2]

    flat = trans[...].reshape(KINDS * PATCH, PATCH)
    t_hi, t_low = split2(flat)
    tmat[:, 0:PATCH] = t_hi.astype(BF16)
    tmat[:, PATCH : 2 * PATCH] = t_hi.astype(BF16)
    tmat[:, 2 * PATCH : 3 * PATCH] = t_low.astype(BF16)

    def transit_chunk(j):
        for kk in range(CHUNK):
            k = j * CHUNK + kk
            hi, low = split2(grown[pl.ds(pl.multiple_of(k * PATCH, PATCH), PATCH), :])
            cols = slice(kk * LANES, (kk + 1) * LANES)
            rhs[0:PATCH, cols] = hi.astype(BF16)
            rhs[PATCH : 2 * PATCH, cols] = low.astype(BF16)
            rhs[2 * PATCH : 3 * PATCH, cols] = hi.astype(BF16)
        moved = nn_dot(tmat[...], rhs[...])
        for kk in range(CHUNK):
            cols = slice(kk * LANES, (kk + 1) * LANES)
            total = moved[0:PATCH, cols] * weight[0:1, :]
            for kind in range(1, KINDS):
                total += moved[kind * PATCH : (kind + 1) * PATCH, cols] * weight[kind : kind + 1, :]
            tr_out[pl.ds(j * CHUNK + kk, PATCH, stride=BINS), :] = total

    lane16 = lax.broadcasted_iota(jnp.int32, (ROWS, LANES), 1)
    stride = step[...]
    dest = jnp.where(stride > 0, sub16 * LANES + lane16 + stride, -1)
    dest_lane = dest & (LANES - 1)
    dest_row = dest >> 7
    sub32 = lax.broadcasted_iota(jnp.int32, (32, LANES), 0)
    for c in range(ROWS):
        hot = jnp.where(sub128 == dest_lane[c : c + 1, :], 1.0, 0.0)
        lane_step[c * LANES : (c + 1) * LANES, :] = hot.T.astype(BF16)
        row_step[:, c * LANES : (c + 1) * LANES] = jnp.where(sub32 == dest_row[c : c + 1, :], 1.0, 0.0).astype(BF16)

    listed = jnp.zeros((8, LANES), jnp.int32)
    for a in range(NA):
        row = jnp.broadcast_to(tgt[a // 2 : a // 2 + 1, :], (8, LANES))
        row = pltpu.roll(row, ((a - (a % 2) * 8) * 8) % LANES, 1)
        listed = jnp.where(((block8 - sub8) & 15) == a, row, listed)
    for bit in (1, 2, 4):
        listed = jnp.where((sub8 & bit) != 0, pltpu.roll(listed, LANES - bit * 8, 1), listed)
    list_lane = listed & (LANES - 1)
    list_row = listed >> 7
    for b in range(NB):
        cols = slice(b * LANES, (b + 1) * LANES)
        lane_rcv[:, cols] = jnp.where(sub128 == list_lane[b : b + 1, :], 1.0, 0.0).astype(BF16)
        row_rcv[:, cols] = jnp.where(sub16 == list_row[b : b + 1, :], 1.0, 0.0)

    for c in range(ROWS):
        cols = slice(c * LANES, (c + 1) * LANES)
        for q in range(4):
            state[q, c : c + 1, :] = water[q : q + 1, cols]
            state[4 + q, c : c + 1, :] = rates[q : q + 1, cols]
    transit_chunk(0)
    transit_chunk(1)

    each(NA, lambda k: arrive_a(k).wait_recv())
    half = my_a % 2
    tiles = []
    for a in range(NA):
        tiles.append(pltpu.roll(recv_a[a], (half * 64 + a * 8) % LANES, 1))
    for b in range(NB):
        mixed = jnp.zeros((8, LANES), F32)
        for a in range(NA):
            mixed = jnp.where(block8 == (a + b) % 16, tiles[a], mixed)
        send_b[b] = pltpu.roll(mixed, (LANES - b * 8) % LANES, 1)
    each(NB, lambda k: copy_b(k).start())
    recv_b[my_b] = send_b[my_b]
    transit_chunk(2)
    transit_chunk(3)
    each(NB, lambda k: arrive_b(k).wait_recv())

    for b in range(NB):
        cols = slice(b * LANES, (b + 1) * LANES)
        hot = row_rcv[:, cols]
        for s, part in enumerate(split3(recv_b[b])):
            for f in range(3):
                lhs_rcv[(s * 3 + f) * ROWS : (s * 3 + f + 1) * ROWS, cols] = (part[f : f + 1, :] * hot).astype(BF16)
    landed = nt_dot(lhs_rcv[...], lane_rcv[...])
    landed = (landed[0:48] + landed[48:96] + landed[96:144]) * (1.0 / NSUB)
    surface = (landed[0:ROWS], landed[ROWS : 2 * ROWS])
    deep = (landed[2 * ROWS : 3 * ROWS], jnp.zeros((ROWS, LANES), F32))

    def substep(t, carry):
        hill, channel = carry[0:2], carry[2:4]
        partial, hill_next = [], []
        for q in range(2):
            hill_out = state[4 + q] * hill[q]
            outflow = state[6 + q] * channel[q]
            partial.append(channel[q] - outflow + hill_out + deep[q])
            hill_next.append(hill[q] - hill_out + surface[q])
            for s, part in enumerate(split2(outflow)):
                rows = slice((q * 2 + s) * 32, (q * 2 + s + 1) * 32)
                for c in range(ROWS):
                    cols = slice(c * LANES, (c + 1) * LANES)
                    value = jnp.broadcast_to(part[c : c + 1, :], (32, LANES)).astype(BF16)
                    lhs_step[rows, cols] = value * row_step[:, cols]
        spread = nn_dot(lhs_step[...], lane_step[...])
        sums = []
        for q in range(2):
            both = spread[q * 64 : q * 64 + 32] + spread[q * 64 + 32 : q * 64 + 64]
            send_ring[t, q] = both[ROWS:]
            sums.append(both[:ROWS])
        copy = ring(t)
        copy.start()
        transit_chunk(t + 4)
        copy.wait_recv()
        new = [partial[q] + sums[q] + recv_ring[t, q] for q in range(2)]
        return (*hill_next, *new)

    final = lax.fori_loop(0, NSUB, substep, tuple(state[q] for q in range(4)))
    stored = final[2] + final[3]
    inundation = stored / (stored + cap[...])
    lhs = jnp.concatenate(split3(inundation), axis=0).astype(BF16)
    seen = nn_dot(lhs, lane_rcv[...])
    seen = (seen[0:16] + seen[16:32] + seen[32:48]) * row_rcv[...]
    for b in range(NB):
        row = jnp.sum(seen[:, b * LANES : (b + 1) * LANES], axis=0, keepdims=True)
        send_rb[b] = jnp.broadcast_to(row, (8, LANES))
    each(NB, lambda k: copy_rb(k).start())
    recv_rb[my_b] = send_rb[my_b]
    for c in range(ROWS):
        cols = slice(c * LANES, (c + 1) * LANES)
        for q in range(4):
            river_out[q : q + 1, cols] = final[q][c : c + 1, :]
    each(NB, lambda k: arrive_rb(k).wait_recv())
    gathered = jnp.zeros((8, LANES), F32)
    for b in range(NB):
        gathered = jnp.where(sub8 == b, recv_rb[b], gathered)
    send_ra[...] = gathered
    each(NA, lambda k: copy_ra(k).start())
    recv_ra[my_a] = gathered
    each(NA, lambda k: arrive_ra(k).wait_recv())
    for r in range(8):
        even = pltpu.roll(recv_ra[2 * r], (LANES - my_a * 8) % LANES, 1)
        odd = pltpu.roll(recv_ra[2 * r + 1], (64 + LANES - my_a * 8) % LANES, 1)
        pair = jnp.where(lane8 < 64, even, odd)
        for bit in (1, 2, 4):
            pair = jnp.where((sub8 & bit) != 0, pltpu.roll(pair, bit * 8, 1), pair)
        row = jnp.sum(jnp.where((block8 & 7) == sub8, pair, 0.0), axis=0, keepdims=True) * share[r : r + 1, :]
        hi, mid, low = split3(row)
        tile = jnp.where(sub16 == 0, hi, jnp.where(sub16 == 1, mid, jnp.where(sub16 == 2, low, 0.0)))
        lhs_back[:, r * LANES : (r + 1) * LANES] = tile.astype(BF16)
    felt = nt_dot(lhs_back[...], onehot_src[...])
    flood_out[...] = felt[0:1] + felt[1:2] + felt[2:3]

    each(NA, lambda k: copy_a(k).wait_send())
    each(NB, lambda k: copy_b(k).wait_send())
    each(NB, lambda k: copy_rb(k).wait_send())
    each(NA, lambda k: copy_ra(k).wait_send())

    def ring_done(t, _):
        ring(t).wait_send()
        return 0

    lax.fori_loop(0, NSUB, ring_done, 0)


def survive_kernel(mass, traits, flooded, out, survival):
    @pl.when(pl.program_id(0) == 0)
    def _():
        rows = lax.broadcasted_iota(jnp.int32, (BINS, BINS), 0)
        cols = lax.broadcasted_iota(jnp.int32, (BINS, BINS), 1)
        mortality = jnp.sum(jnp.where(rows == cols, traits[3:4, :], 0.0), axis=1, keepdims=True)
        survival[...] = jnp.exp(-mortality * flooded[...])

    for p in range(mass.shape[0] // BINS):
        rows = slice(p * BINS, (p + 1) * BINS)
        out[rows, :] = mass[rows, :] * survival[...]


def shards(
    biomass, patch_area, cohort_traits, cell_forcing, disturb_weight, transitions, land_source, pair_share,
    river_target, downstream_step, river_water, river_rates, capacity,
):
    vmem = pl.BlockSpec(memory_space=pltpu.VMEM)
    smem = pl.BlockSpec(memory_space=pltpu.SMEM)
    dma = pltpu.SemaphoreType.DMA
    tile = (8, LANES)
    n_rows = PATCH * BINS
    transited, flooded, river_state = pl.pallas_call(
        main_kernel,
        out_shape=(
            jax.ShapeDtypeStruct((n_rows, LANES), F32),
            jax.ShapeDtypeStruct((1, LANES), F32),
            jax.ShapeDtypeStruct((4, ROWS * LANES), F32),
        ),
        in_specs=[vmem, vmem, smem] + [vmem] * 10,
        out_specs=(vmem, vmem, vmem),
        scratch_shapes=[
            pltpu.VMEM((n_rows, LANES), F32),
            pltpu.VMEM((KINDS * PATCH, 3 * PATCH), BF16),
            pltpu.VMEM((3 * PATCH, CHUNK * LANES), BF16),
            pltpu.VMEM((LANES, 1024), BF16),
            pltpu.VMEM((LANES, 1024), BF16),
            pltpu.VMEM((ROWS, 1024), F32),
            pltpu.VMEM((ROWS * LANES, LANES), BF16),
            pltpu.VMEM((32, ROWS * LANES), BF16),
            pltpu.VMEM((128, ROWS * LANES), BF16),
            pltpu.VMEM((9 * ROWS, 1024), BF16),
            pltpu.VMEM((16, 1024), BF16),
            pltpu.VMEM((8, ROWS, LANES), F32),
            pltpu.VMEM((8, *tile), F32),
            pltpu.VMEM((NA, *tile), F32),
            pltpu.VMEM((NB, *tile), F32),
            pltpu.VMEM((NB, *tile), F32),
            pltpu.VMEM((NB, *tile), F32),
            pltpu.VMEM((NB, *tile), F32),
            pltpu.VMEM(tile, F32),
            pltpu.VMEM((NA, *tile), F32),
            pltpu.VMEM((NSUB, 2, ROWS, LANES), F32),
            pltpu.VMEM((NSUB, 2, ROWS, LANES), F32),
            dma((NA,)), dma((NA,)), dma((NB,)), dma((NB,)), dma((NB,)), dma((NB,)), dma((NA,)), dma((NA,)),
            dma((NSUB,)), dma((NSUB,)),
        ],
        compiler_params=pltpu.CompilerParams(
            collective_id=0, has_side_effects=True, vmem_limit_bytes=40 * 1024 * 1024),
        name="hour",
    )(
        biomass.reshape(n_rows, LANES), patch_area, cohort_traits, cell_forcing, disturb_weight, transitions,
        land_source.reshape(8, LANES), pair_share.reshape(8, LANES), river_target.reshape(8, LANES),
        downstream_step.reshape(ROWS, LANES), river_water, river_rates, capacity.reshape(ROWS, LANES),
    )
    block = 8 * BINS
    new_biomass = pl.pallas_call(
        survive_kernel,
        grid=(n_rows // block,),
        out_shape=jax.ShapeDtypeStruct((n_rows, LANES), F32),
        in_specs=[
            pl.BlockSpec((block, LANES), lambda i: (i, 0)),
            pl.BlockSpec((4, BINS), lambda i: (0, 0)),
            pl.BlockSpec((1, LANES), lambda i: (0, 0)),
        ],
        out_specs=pl.BlockSpec((block, LANES), lambda i: (i, 0)),
        scratch_shapes=[pltpu.VMEM((BINS, LANES), F32)],
        name="survive",
    )(transited, cohort_traits, flooded)
    return new_biomass.reshape(PATCH, BINS, LANES), flooded.reshape(LANES), river_state


def solution(mesh):
    both = ("comp", "cell")
    return jax.shard_map(
        shards,
        mesh=mesh,
        in_specs=(
            P(None, None, both), P(None, both), P(), P(None, both), P(None, both), P(), P(both), P(both), P(both),
            P(both), P(None, both), P(None, both), P(both),
        ),
        out_specs=(P(None, None, both), P(both), P(None, both)),
        check_vma=False,
    )
```

time: 401 us -> 71.7 us (0.18)
  other arithmetic: 217 us -> 0 us
  local copies, waits for them, and re-layouts: 101 us -> 12.9 us
  starting transfers between devices: 58.1 us -> 0 us
  Pallas kernels: 0 us -> 57.5 us
  matrix products: 17.1 us -> 0 us
    scatter-add x14 -> x0, other arithmetic: 163 us -> none  [the longest x12 149 us: scatter_pair(): return jax.ops.segment_sum(outflow.T, slots, num_segments=segments).T]
    pallas_call x0 -> x2, Pallas kernels: none -> 57.5 us  [the longest x1 52.9 us: shards(): pl.pallas_call(main_kernel, out_shape=(jax.ShapeDtypeStruct((n_rows, LANE...]
    add x37 -> x0, other arithmetic: 43.5 us -> none  [the longest x12 41.2 us: substep(): hill_water - hill_out + surface_in]
    slice x39 -> x0, local copies, waits for them, and re-layouts: 40.9 us -> none  [the longest x24 36.8 us: substep(): from_above = from_behind(spread[:, rivers:2 * rivers], ('comp', 'cell'), 1)]
    ppermute x12 -> x0, starting transfers between devices: 32.8 us -> none  [from_behind(): lax.ppermute(value, axis, [(source, source + steps) for source in range(i...]
    all_to_all x3 -> x0, starting transfers between devices: 25.4 us -> none  [the longest x1 11.5 us: joined_exchange(): lax.all_to_all(blocks, axis, split_axis=0, concat_axis=0, tiled=True)]
    sub x12 -> x0, local copies, waits for them, and re-layouts: 19.7 us -> none  [substep(): channel - outflow + hill_out + inflow + deep_in]
    dot_general x5 -> x0, matrix products: 17.1 us -> none  [the longest x4 13.5 us: transit(): jnp.dot(transitions[kind_index], flat_mass, precision=highest, preferred_...]
  transfers between devices with their start and end apart: 15 -> 0, of which waited for: 1 -> 0; matrix products, arithmetic and copies ran while one was open for 24% -> 0% of each run, Pallas kernels for 0% -> 0%
where the time goes in v1:
time: 71.7 us; the launch traced here: 71 us
  Pallas kernels  57.5 us (80%)
  local copies, waits for them, and re-layouts  12.9 us (18%)
    pallas_call x1, Pallas kernels, shards(): pl.pallas_call(main_kernel, out_shape=(jax.ShapeDtypeStruct((n_rows, LANE...  52.9 us
    unnamed x34, local copies, waits for them, and re-layouts  12.9 us
    pallas_call x1, Pallas kernels, shards(): pl.pallas_call(survive_kernel, grid=(n_rows // block,), out_shape=jax.Sha...  4.65 us

profile of v1, /device:TPU:1, one launch (start us, length us, event | category | flops | bytes accessed | tf_op | source)
XLA Modules:
  0.0 71.0 jit_solution(5245930251835855282)
XLA Ops:
  0.6 0.0 copy-start
  0.6 1.4 %copy-done = f32[48,64,128]{2,1,0:T(8,128)S(1)} copy-done((f32[48,64,128]{2,1,0:T(8,128)S(1)}, f32[48,64,128]{2,1,0:T(8,128)}, u32[]{:S(2)}) %copy-start) | copy-done | bytes 1572888
  2.0 0.0 copy-start.2
  2.0 0.9 %copy-done.2 = f32[4,48,48]{2,1,0:T(8,128)S(1)} copy-done((f32[4,48,48]{2,1,0:T(8,128)S(1)}, f32[4,48,48]{2,1,0:T(8,128)}, u32[]{:S(2)}) %copy-start.2) | copy-done | bytes 36888
  2.9 0.0 copy-start.3
  2.9 0.8 %copy-done.3 = f32[4,2048]{1,0:T(4,128)S(1)} copy-done((f32[4,2048]{1,0:T(4,128)S(1)}, f32[4,2048]{1,0:T(4,128)}, u32[]{:S(2)}) %copy-start.3) | copy-done | bytes 32792
  3.7 0.8 %copy-done.4 = f32[4,2048]{1,0:T(4,128)S(1)} copy-done((f32[4,2048]{1,0:T(4,128)S(1)}, f32[4,2048]{1,0:T(4,128)}, u32[]{:S(2)}) %copy-start.4) | copy-done | bytes 32792
  4.5 0.7 %copy-done.5 = f32[48,128]{1,0:T(8,128)S(1)} copy-done((f32[48,128]{1,0:T(8,128)S(1)}, f32[48,128]{1,0:T(8,128)}, u32[]{:S(2)}) %copy-start.5) | copy-done | bytes 24600
  5.2 0.7 copy-done.6
  5.9 0.7 copy-done.7
  6.6 0.7 copy-done.8
  7.3 0.7 copy-done.9
  8.0 0.7 copy-done.10
  8.6 0.7 copy-done.11
  9.3 0.7 copy-done.12
  10.0 0.7 copy-done.13
  10.7 52.9 %hour.1 = (f32[3072,128]{1,0:T(8,128)S(1)}, f32[1,128]{1,0:T(1,128)S(1)}, f32[4,2048]{1,0:T(4,128)S(1)}) custom-call(f32[3072,128]{1,0:T(8,128)S(1)} %bitcast.8, f32[48,128]{1,0:T(8,128)S(1)} %copy-done.5, f32[4,64]{1,0:T(4,128)S(1)} %copy-done.8, f32[5,128]{1,0:T(8,128)S(1)} %copy-done.9, f32[4,128]{1,0:T(4,128)S(1)} %copy-done.13, ...), custom_call_target="tpu_custom_call" | custom-call | tf_op jit(solution)/shard_map/hour/pallas_call | solution.py:359
  63.6 0.0 copy-start.1
  63.6 1.2 %copy-done.1 = f32[3072,128]{1,0:T(8,128)} copy-done((f32[3072,128]{1,0:T(8,128)}, f32[3072,128]{1,0:T(8,128)S(1)}, u32[]{:S(2)}) %copy-start.1) | copy-done | bytes 1572888
  64.7 0.5 copy-done.14
  65.3 4.6 %survive.1 = f32[3072,128]{1,0:T(8,128)} custom-call(f32[3072,128]{1,0:T(8,128)} %copy-done.1, f32[4,64]{1,0:T(4,128)} %traits.3, f32[1,128]{1,0:T(1,128)} %copy-done.14), custom_call_target="tpu_custom_call" | custom-call | tf_op jit(solution)/shard_map/survive/pallas_call | solution.py:403
  69.9 0.0 copy-done.15
  69.9 0.5 copy.18
  70.4 0.6 copy.19
  (12 shorter events, 0.0 us)
Async XLA Ops:
  0.6 1.4 %copy-start = (f32[48,64,128]{2,1,0:T(8,128)S(1)}, f32[48,64,128]{2,1,0:T(8,128)}, u32[]{:S(2)}) copy-start(f32[48,64,128]{2,1,0:T(8,128)} %param.13) | copy-start | bytes 4718596
  2.0 0.9 %copy-start.2 = (f32[4,48,48]{2,1,0:T(8,128)S(1)}, f32[4,48,48]{2,1,0:T(8,128)}, u32[]{:S(2)}) copy-start(f32[4,48,48]{2,1,0:T(8,128)} %trans.1) | copy-start | bytes 110596
  2.9 0.8 %copy-start.3 = (f32[4,2048]{1,0:T(4,128)S(1)}, f32[4,2048]{1,0:T(4,128)}, u32[]{:S(2)}) copy-start(f32[4,2048]{1,0:T(4,128)} %water.1) | copy-start | bytes 98308
  3.7 0.8 %copy-start.4 = (f32[4,2048]{1,0:T(4,128)S(1)}, f32[4,2048]{1,0:T(4,128)}, u32[]{:S(2)}) copy-start(f32[4,2048]{1,0:T(4,128)} %rates.1) | copy-start | bytes 98308
  4.5 0.7 %copy-start.5 = (f32[48,128]{1,0:T(8,128)S(1)}, f32[48,128]{1,0:T(8,128)}, u32[]{:S(2)}) copy-start(f32[48,128]{1,0:T(8,128)} %area.1) | copy-start | bytes 73732
  5.2 0.7 copy-start.6
  5.9 0.7 copy-start.7
  6.6 0.7 copy-start.8
  7.3 0.7 copy-start.9
  8.0 0.7 copy-start.10
  8.6 0.7 copy-start.11
  9.3 0.7 copy-start.12
  10.0 0.7 copy-start.13
  63.6 1.2 %copy-start.1 = (f32[3072,128]{1,0:T(8,128)}, f32[3072,128]{1,0:T(8,128)S(1)}, u32[]{:S(2)}) copy-start(f32[3072,128]{1,0:T(8,128)S(1)} %get-tuple-element.6.mass) | copy-start | bytes 4718596
  64.7 0.5 copy-start.14
  65.2 4.7 %copy-start.15 = (f32[1,128]{1,0:T(1,128)S(1)}, f32[1,128]{1,0:T(1,128)}, u32[]{:S(2)}) copy-start(f32[1,128]{1,0:T(1,128)} %copy-done.14) | copy-start | bytes 1540

commit v2 on v1

--- a/solution.py
+++ b/solution.py
@@ -40,12 +40,27 @@
 
 
 def main_kernel(
-    bio, area, traits, forcing, weight, trans, src, share, tgt, step, water, rates, cap,
-    tr_out, flood_out, river_out,
+    bio_in, area_in, traits_in, forcing_in, weight_in, trans_in, src_in, share_in, tgt_in, step_in, water_in, rates_in,
+    cap_in,
+    tr_hbm, flood_hbm, river_hbm,
+    tr_out, flood_out, river_out, out_sem,
+    bio, area, traits, forcing, weight, trans, src, share, tgt, step, water, rates, cap, in_sem, bio_sem,
     grown, tmat, rhs, onehot_src, lane_rcv, row_rcv, lane_step, row_step, lhs_step, lhs_rcv, lhs_back, state,
     send_a, recv_a, send_b, recv_b, send_rb, recv_rb, send_ra, recv_ra, send_ring, recv_ring,
     sa_s, sa_r, sb_s, sb_r, rb_s, rb_r, ra_s, ra_r, ring_s, ring_r,
 ):
+    sources = (area_in, traits_in, forcing_in, weight_in, trans_in, src_in, share_in, tgt_in, step_in, water_in, rates_in, cap_in)
+    targets = (area, traits, forcing, weight, trans, src, share, tgt, step, water, rates, cap)
+    loads = [pltpu.make_async_copy(sources[i], targets[i], in_sem.at[i]) for i in range(12)]
+    for i in (5, 1, 2):
+        loads[i].start()
+    mass_loads = [
+        pltpu.make_async_copy(bio_in.at[:, pl.ds(g * 8, 8), :], bio.at[g], bio_sem.at[g]) for g in range(BINS // 8)
+    ]
+    for g in range(BINS // 8 - 1, -1, -1):
+        mass_loads[g].start()
+    for i in (0, 6, 4, 3, 8, 7, 9, 10, 11):
+        loads[i].start()
     my_x = lax.axis_index("comp")
     cell = lax.axis_index("cell")
     my_y, my_b = cell // NB, cell % NB
@@ -81,24 +96,35 @@
     sub16 = lax.broadcasted_iota(jnp.int32, (16, LANES), 0)
     sub128 = lax.broadcasted_iota(jnp.int32, (LANES, LANES), 0)
 
+    loads[5].wait()
     for r in range(8):
         hot = jnp.where(sub128 == src[r : r + 1, :], 1.0, 0.0)
         onehot_src[:, r * LANES : (r + 1) * LANES] = hot.astype(BF16)
 
+    loads[1].wait()
+    loads[2].wait()
     light = forcing[0:1, :]
     light_factor = light / (light + 0.5)
 
-    def canopy_bin(i, carry):
-        above, total = carry
-        k = BINS - 1 - i
-        mass = bio[pl.ds(k, PATCH, stride=BINS), :]
-        leaf = mass * traits[0, k]
-        gain = (traits[1, k] * light_factor) * leaf * jnp.exp(-0.05 * above)
-        grown[pl.ds(pl.multiple_of(k * PATCH, PATCH), PATCH), :] = mass * (1.0 - 0.1 * traits[2, k]) + 0.5 * gain
-        return above + leaf, total + gain
-
     zero48 = jnp.zeros((PATCH, LANES), F32)
-    _, total = lax.fori_loop(0, BINS, canopy_bin, (zero48, zero48), unroll=4)
+    carry = (zero48, zero48)
+    for g in range(BINS // 8 - 1, -1, -1):
+        mass_loads[g].wait()
+        group = bio.at[g].reshape(PATCH * 8, LANES)
+
+        def canopy_bin(i, carry, g=g, group=group):
+            above, total = carry
+            kk = 7 - i
+            k = g * 8 + kk
+            mass = group[pl.ds(kk, PATCH, stride=8), :]
+            leaf = mass * traits[0, k]
+            gain = (traits[1, k] * light_factor) * leaf * jnp.exp(-0.05 * above)
+            grown[pl.ds(pl.multiple_of(k * PATCH, PATCH), PATCH), :] = mass * (1.0 - 0.1 * traits[2, k]) + 0.5 * gain
+            return above + leaf, total + gain
+
+        carry = lax.fori_loop(0, 8, canopy_bin, carry, unroll=True)
+    total = carry[1]
+    loads[0].wait()
     transpiration = 0.5 * jnp.sum(area[...] * total, axis=0, keepdims=True)
     wet = forcing[1:2, :] * forcing[2:3, :]
     frozen = forcing[4:5, :]
@@ -108,6 +134,7 @@
     runoff = jnp.where(sub8 == 0, row0, jnp.where(sub8 == 1, row1, jnp.where(sub8 == 2, row2, 0.0)))
     parts = split3(runoff)
     lhs = jnp.concatenate([*parts, jnp.zeros((8, LANES), F32)], axis=0).astype(BF16)
+    loads[6].wait()
     picked = nn_dot(lhs, onehot_src[...])
     picked = picked[0:8] + picked[8:16] + picked[16:24]
     for r in range(8):
@@ -177,6 +204,8 @@
     each(NA, lambda k: copy_a(k).start())
     recv_a[my_a] = send_a[my_a // 2]
 
+    for i in (4, 3, 8, 7, 9, 10, 11):
+        loads[i].wait()
     flat = trans[...].reshape(KINDS * PATCH, PATCH)
     t_hi, t_low = split2(flat)
     tmat[:, 0:PATCH] = t_hi.astype(BF16)
@@ -301,6 +330,12 @@
         cols = slice(c * LANES, (c + 1) * LANES)
         for q in range(4):
             river_out[q : q + 1, cols] = final[q][c : c + 1, :]
+    stores = (
+        pltpu.make_async_copy(tr_out, tr_hbm, out_sem.at[0]),
+        pltpu.make_async_copy(river_out, river_hbm, out_sem.at[1]),
+    )
+    for copy in stores:
+        copy.start()
     each(NB, lambda k: arrive_rb(k).wait_recv())
     gathered = jnp.zeros((8, LANES), F32)
     for b in range(NB):
@@ -321,6 +356,8 @@
         lhs_back[:, r * LANES : (r + 1) * LANES] = tile.astype(BF16)
     felt = nt_dot(lhs_back[...], onehot_src[...])
     flood_out[...] = felt[0:1] + felt[1:2] + felt[2:3]
+    store = pltpu.make_async_copy(flood_out, flood_hbm, out_sem.at[2])
+    store.start()
 
     each(NA, lambda k: copy_a(k).wait_send())
     each(NB, lambda k: copy_b(k).wait_send())
@@ -332,27 +369,50 @@
         return 0
 
     lax.fori_loop(0, NSUB, ring_done, 0)
-
-
-def survive_kernel(mass, traits, flooded, out, survival):
-    @pl.when(pl.program_id(0) == 0)
-    def _():
-        rows = lax.broadcasted_iota(jnp.int32, (BINS, BINS), 0)
-        cols = lax.broadcasted_iota(jnp.int32, (BINS, BINS), 1)
-        mortality = jnp.sum(jnp.where(rows == cols, traits[3:4, :], 0.0), axis=1, keepdims=True)
-        survival[...] = jnp.exp(-mortality * flooded[...])
-
-    for p in range(mass.shape[0] // BINS):
-        rows = slice(p * BINS, (p + 1) * BINS)
-        out[rows, :] = mass[rows, :] * survival[...]
+    for copy in (*stores, store):
+        copy.wait()
+
+
+def survive_kernel(
+    mass_in, traits_in, flooded_in, river_in, out, flooded_out, river_out,
+    mass, traits, flooded, survival, load_sem, store_sem,
+):
+    block = PATCH * BINS // 6
+    small = [
+        pltpu.make_async_copy(flooded_in, flooded, load_sem.at[6]),
+        pltpu.make_async_copy(traits_in, traits, load_sem.at[7]),
+    ]
+    pieces = [pl.ds(i * block, block) for i in range(6)]
+    loads = [pltpu.make_async_copy(mass_in.at[p, :], mass.at[p, :], load_sem.at[i]) for i, p in enumerate(pieces)]
+    stores = [pltpu.make_async_copy(mass.at[p, :], out.at[p, :], store_sem.at[i]) for i, p in enumerate(pieces)]
+    stores += [
+        pltpu.make_async_copy(flooded, flooded_out, store_sem.at[6]),
+        pltpu.make_async_copy(river_in, river_out, store_sem.at[7]),
+    ]
+    for copy in (*small, *loads, stores[7]):
+        copy.start()
+    for copy in small:
+        copy.wait()
+    stores[6].start()
+    rows = lax.broadcasted_iota(jnp.int32, (BINS, BINS), 0)
+    cols = lax.broadcasted_iota(jnp.int32, (BINS, BINS), 1)
+    mortality = jnp.sum(jnp.where(rows == cols, traits[3:4, :], 0.0), axis=1, keepdims=True)
+    survival[...] = jnp.exp(-mortality * flooded[...])
+    for i in range(6):
+        loads[i].wait()
+        for p in range(8):
+            rows = slice(i * block + p * BINS, i * block + (p + 1) * BINS)
+            mass[rows, :] = mass[rows, :] * survival[...]
+        stores[i].start()
+    for copy in stores:
+        copy.wait()
 
 
 def shards(
     biomass, patch_area, cohort_traits, cell_forcing, disturb_weight, transitions, land_source, pair_share,
     river_target, downstream_step, river_water, river_rates, capacity,
 ):
-    vmem = pl.BlockSpec(memory_space=pltpu.VMEM)
-    smem = pl.BlockSpec(memory_space=pltpu.SMEM)
+    hbm = pl.BlockSpec(memory_space=pltpu.HBM)
     dma = pltpu.SemaphoreType.DMA
     tile = (8, LANES)
     n_rows = PATCH * BINS
@@ -363,9 +423,28 @@
             jax.ShapeDtypeStruct((1, LANES), F32),
             jax.ShapeDtypeStruct((4, ROWS * LANES), F32),
         ),
-        in_specs=[vmem, vmem, smem] + [vmem] * 10,
-        out_specs=(vmem, vmem, vmem),
+        in_specs=[hbm] * 13,
+        out_specs=(hbm, hbm, hbm),
         scratch_shapes=[
+            pltpu.VMEM((n_rows, LANES), F32),
+            pltpu.VMEM((1, LANES), F32),
+            pltpu.VMEM((4, ROWS * LANES), F32),
+            dma((3,)),
+            pltpu.VMEM((BINS // 8, PATCH, 8, LANES), F32),
+            pltpu.VMEM((PATCH, LANES), F32),
+            pltpu.SMEM((4, BINS), F32),
+            pltpu.VMEM((5, LANES), F32),
+            pltpu.VMEM((KINDS, LANES), F32),
+            pltpu.VMEM((KINDS, PATCH, PATCH), F32),
+            pltpu.VMEM(tile, jnp.int32),
+            pltpu.VMEM(tile, F32),
+            pltpu.VMEM(tile, jnp.int32),
+            pltpu.VMEM((ROWS, LANES), jnp.int32),
+            pltpu.VMEM((4, ROWS * LANES), F32),
+            pltpu.VMEM((4, ROWS * LANES), F32),
+            pltpu.VMEM((ROWS, LANES), F32),
+            dma((12,)),
+            dma((BINS // 8,)),
             pltpu.VMEM((n_rows, LANES), F32),
             pltpu.VMEM((KINDS * PATCH, 3 * PATCH), BF16),
             pltpu.VMEM((3 * PATCH, CHUNK * LANES), BF16),
@@ -392,27 +471,33 @@
             dma((NSUB,)), dma((NSUB,)),
         ],
         compiler_params=pltpu.CompilerParams(
-            collective_id=0, has_side_effects=True, vmem_limit_bytes=40 * 1024 * 1024),
+            collective_id=0, has_side_effects=True, vmem_limit_bytes=60 * 1024 * 1024),
         name="hour",
     )(
-        biomass.reshape(n_rows, LANES), patch_area, cohort_traits, cell_forcing, disturb_weight, transitions,
+        biomass, patch_area, cohort_traits, cell_forcing, disturb_weight, transitions,
         land_source.reshape(8, LANES), pair_share.reshape(8, LANES), river_target.reshape(8, LANES),
         downstream_step.reshape(ROWS, LANES), river_water, river_rates, capacity.reshape(ROWS, LANES),
     )
-    block = 8 * BINS
-    new_biomass = pl.pallas_call(
+    new_biomass, flooded, river_state = pl.pallas_call(
         survive_kernel,
-        grid=(n_rows // block,),
-        out_shape=jax.ShapeDtypeStruct((n_rows, LANES), F32),
-        in_specs=[
-            pl.BlockSpec((block, LANES), lambda i: (i, 0)),
-            pl.BlockSpec((4, BINS), lambda i: (0, 0)),
-            pl.BlockSpec((1, LANES), lambda i: (0, 0)),
+        out_shape=(
+            jax.ShapeDtypeStruct((n_rows, LANES), F32),
+            jax.ShapeDtypeStruct((1, LANES), F32),
+            jax.ShapeDtypeStruct((4, ROWS * LANES), F32),
+        ),
+        in_specs=[hbm] * 4,
+        out_specs=(hbm, hbm, hbm),
+        scratch_shapes=[
+            pltpu.VMEM((n_rows, LANES), F32),
+            pltpu.VMEM((4, BINS), F32),
+            pltpu.VMEM((1, LANES), F32),
+            pltpu.VMEM((BINS, LANES), F32),
+            dma((8,)),
+            dma((8,)),
         ],
-        out_specs=pl.BlockSpec((block, LANES), lambda i: (i, 0)),
-        scratch_shapes=[pltpu.VMEM((BINS, LANES), F32)],
+        compiler_params=pltpu.CompilerParams(vmem_limit_bytes=60 * 1024 * 1024),
         name="survive",
-    )(transited, cohort_traits, flooded)
+    )(transited, cohort_traits, flooded, river_state)
     return new_biomass.reshape(PATCH, BINS, LANES), flooded.reshape(LANES), river_state
 
 

time: 71.7 us -> 55.8 us (0.78)
  local copies, waits for them, and re-layouts: 12.9 us -> 0 us
  Pallas kernels: 57.5 us -> 55 us
    unnamed x34 -> x0, local copies, waits for them, and re-layouts: 12.9 us -> none
    pallas_call x1, Pallas kernels: 4.65 us -> 2.27 us  [shards(): pl.pallas_call(survive_kernel, out_shape=(jax.ShapeDtypeStruct((n_rows, L...]
where the time goes in v2:
time: 55.8 us; the launch traced here: 55.6 us
  Pallas kernels  55 us (99%)
  between operations  0.64 us (1%)
    pallas_call x1, Pallas kernels, shards(): pl.pallas_call(main_kernel, out_shape=(jax.ShapeDtypeStruct((n_rows, LANE...  52.7 us
    pallas_call x1, Pallas kernels, shards(): pl.pallas_call(survive_kernel, out_shape=(jax.ShapeDtypeStruct((n_rows, L...  2.27 us

profile of v2, /device:TPU:1, one launch (start us, length us, event | category | flops | bytes accessed | tf_op | source)
XLA Modules:
  0.0 55.6 jit_solution(14177810354830609325)
XLA Ops:
  0.6 52.7 %hour.1 = (f32[3072,128]{1,0:T(8,128)}, f32[1,128]{1,0:T(1,128)}, f32[4,2048]{1,0:T(4,128)}) custom-call(f32[48,64,128]{2,1,0:T(8,128)} %bio_in.1, f32[48,128]{1,0:T(8,128)} %area_in.1, f32[4,64]{1,0:T(4,128)} %traits_in.3, f32[5,128]{1,0:T(8,128)} %forcing_in.1, f32[4,128]{1,0:T(4,128)} %weight_in.1, f32[4,48,48]{2,1,0:T(8,128)} %trans_in.1, ...), custom_call_target="tpu_custom_call" | custom-call | tf_op jit(solution)/shard_map/hour/pallas_call | solution.py:419
  53.4 2.3 %survive.1 = (f32[3072,128]{1,0:T(8,128)}, f32[1,128]{1,0:T(1,128)}, f32[4,2048]{1,0:T(4,128)}) custom-call(f32[3072,128]{1,0:T(8,128)} %get-tuple-element.9.mass_in, f32[4,64]{1,0:T(4,128)} %traits_in.3, f32[1,128]{1,0:T(1,128)} %get-tuple-element.10.flooded_in, f32[4,2048]{1,0:T(4,128)} %get-tuple-element.11.river_in), custom_call_target="tpu_custom_call" | custom-call | tf_op jit(solution)/shard_map/survive/pallas_call | solution.py:481

commit v3 on v2

--- a/solution.py
+++ b/solution.py
@@ -18,6 +18,11 @@
 NB = 8
 ROWS = 16
 CHUNK = 4
+G = 4
+STEPS = NSUB // G
+CHUNKS_STEP = 12 // STEPS
+A_PATHS = 3
+OFF = [ROWS * sum(j + 1 for j in range(1, k)) for k in range(1, G + 2)]
 
 
 def split2(x):
@@ -46,6 +51,7 @@
     tr_out, flood_out, river_out, out_sem,
     bio, area, traits, forcing, weight, trans, src, share, tgt, step, water, rates, cap, in_sem, bio_sem,
     grown, tmat, rhs, onehot_src, lane_rcv, row_rcv, lane_step, row_step, lhs_step, lhs_rcv, lhs_back, state,
+    moved_by, table, table_send, path, path_rate, st_s, st_r,
     send_a, recv_a, send_b, recv_b, send_rb, recv_rb, send_ra, recv_ra, send_ring, recv_ring,
     sa_s, sa_r, sb_s, sb_r, rb_s, rb_r, ra_s, ra_r, ring_s, ring_r,
 ):
@@ -66,8 +72,6 @@
     my_y, my_b = cell // NB, cell % NB
     my_a = my_x * 4 + my_y
     me = my_x * 32 + cell
-    nxt = (me + 1) % 128
-    prv = (me + 127) % 128
 
     def peer_a(other):
         return (other // 4, (other % 4) * NB + my_b)
@@ -87,8 +91,9 @@
 
     lax.fori_loop(1, NA, greet_a, 0)
     lax.fori_loop(1, NB, greet_b, 0)
-    for other in (nxt, prv):
-        pl.semaphore_signal(barrier, inc=1, device_id=(other // 32, other % 32), device_id_type=MESH)
+    for m in range(1, G + 1):
+        for other in ((me + m) % 128, (me + 128 - m) % 128):
+            pl.semaphore_signal(barrier, inc=1, device_id=(other // 32, other % 32), device_id_type=MESH)
 
     sub8 = lax.broadcasted_iota(jnp.int32, (8, LANES), 0)
     lane8 = lax.broadcasted_iota(jnp.int32, (8, LANES), 1)
@@ -188,10 +193,18 @@
             src_ref=send_ra, dst_ref=recv_ra.at[other], send_sem=ra_s.at[k], recv_sem=ra_r.at[other],
             device_id=peer_a(other), device_id_type=MESH)
 
-    def ring(t):
-        return pltpu.make_async_remote_copy(
-            src_ref=send_ring.at[t], dst_ref=recv_ring.at[t], send_sem=ring_s.at[t], recv_sem=ring_r.at[t],
-            device_id=(nxt // 32, nxt % 32), device_id_type=MESH)
+    def ring(e, m):
+        to = (me + m) % 128
+        return pltpu.make_async_remote_copy(
+            src_ref=send_ring.at[e, m - 1], dst_ref=recv_ring.at[e, m - 1],
+            send_sem=ring_s.at[e, m - 1], recv_sem=ring_r.at[e, m - 1],
+            device_id=(to // 32, to % 32), device_id_type=MESH)
+
+    def upstream(m):
+        to = (me + 128 - m) % 128
+        return pltpu.make_async_remote_copy(
+            src_ref=table_send, dst_ref=table.at[m], send_sem=st_s.at[m], recv_sem=st_r.at[m],
+            device_id=(to // 32, to % 32), device_id_type=MESH)
 
     def each(count, action):
         def one(k, _):
@@ -200,11 +213,21 @@
 
         lax.fori_loop(1, count, one, 0)
 
-    pl.semaphore_wait(barrier, NA + NB)
+    pl.semaphore_wait(barrier, NA + NB - 2 + 2 * G)
     each(NA, lambda k: copy_a(k).start())
     recv_a[my_a] = send_a[my_a // 2]
-
-    for i in (4, 3, 8, 7, 9, 10, 11):
+    loads[8].wait()
+    loads[10].wait()
+    for c in range(ROWS):
+        cols = slice(c * LANES, (c + 1) * LANES)
+        for q in range(2):
+            table_send[q, c : c + 1, :] = rates[2 + q : 3 + q, cols]
+    table_send[2] = step[...].astype(F32)
+    for m in range(1, G):
+        upstream(m).start()
+    table[0] = table_send[...]
+
+    for i in (4, 3, 7, 9, 11):
         loads[i].wait()
     flat = trans[...].reshape(KINDS * PATCH, PATCH)
     t_hi, t_low = split2(flat)
@@ -230,14 +253,40 @@
 
     lane16 = lax.broadcasted_iota(jnp.int32, (ROWS, LANES), 1)
     stride = step[...]
-    dest = jnp.where(stride > 0, sub16 * LANES + lane16 + stride, -1)
-    dest_lane = dest & (LANES - 1)
-    dest_row = dest >> 7
-    sub32 = lax.broadcasted_iota(jnp.int32, (32, LANES), 0)
-    for c in range(ROWS):
-        hot = jnp.where(sub128 == dest_lane[c : c + 1, :], 1.0, 0.0)
-        lane_step[c * LANES : (c + 1) * LANES, :] = hot.T.astype(BF16)
-        row_step[:, c * LANES : (c + 1) * LANES] = jnp.where(sub32 == dest_row[c : c + 1, :], 1.0, 0.0).astype(BF16)
+    path[1] = jnp.where(stride > 0, sub16 * LANES + lane16 + stride, -1)
+
+    def follow(k):
+        count = (k + 1) * ROWS
+        sub_rows = lax.broadcasted_iota(jnp.int32, (count, LANES), 0)
+        if k < G:
+            fields = []
+            for f in range(3):
+                hi, low = split2(jnp.concatenate([table[m, f] for m in range(k + 1)], axis=0))
+                fields += [hi, low]
+            lookup = jnp.concatenate(fields, axis=0).astype(BF16)
+
+        def piece(i, _):
+            for j in range(4):
+                c = i * 4 + j
+                cells = path[k, pl.ds(c, 1), :]
+                cols = pl.ds(pl.multiple_of(c * LANES, LANES), LANES)
+                hot = jnp.where(sub128 == (cells & (LANES - 1)), 1.0, 0.0)
+                lane_step[k - 1, cols, :] = hot.T.astype(BF16)
+                rows = jnp.where(sub_rows == (cells >> 7), 1.0, 0.0)
+                row_step[OFF[k - 1] : OFF[k - 1] + count, cols] = rows.astype(BF16)
+                if k < G:
+                    found = nn_dot(lookup, hot.astype(BF16))
+                    values = []
+                    for f in range(3):
+                        both = found[2 * f * count : (2 * f + 1) * count] + found[(2 * f + 1) * count : (2 * f + 2) * count]
+                        values.append(jnp.sum(both * rows, axis=0, keepdims=True))
+                    path_rate[k, 0, pl.ds(c, 1), :] = values[0]
+                    path_rate[k, 1, pl.ds(c, 1), :] = values[1]
+                    hop = (values[2] + 0.5).astype(jnp.int32)
+                    path[k + 1, pl.ds(c, 1), :] = jnp.where(hop > 0, cells + hop, -1)
+            return 0
+
+        lax.fori_loop(0, 4, piece, 0)
 
     listed = jnp.zeros((8, LANES), jnp.int32)
     for a in range(NA):
@@ -258,8 +307,10 @@
         for q in range(4):
             state[q, c : c + 1, :] = water[q : q + 1, cols]
             state[4 + q, c : c + 1, :] = rates[q : q + 1, cols]
-    transit_chunk(0)
-    transit_chunk(1)
+    for m in range(1, G):
+        upstream(m).wait_recv()
+    for k in range(1, A_PATHS):
+        follow(k)
 
     each(NA, lambda k: arrive_a(k).wait_recv())
     half = my_a % 2
@@ -273,8 +324,23 @@
         send_b[b] = pltpu.roll(mixed, (LANES - b * 8) % LANES, 1)
     each(NB, lambda k: copy_b(k).start())
     recv_b[my_b] = send_b[my_b]
-    transit_chunk(2)
-    transit_chunk(3)
+    for k in range(A_PATHS, G + 1):
+        follow(k)
+    for q in range(2):
+        rate = [table[0, q]] + [path_rate[k, q] for k in range(1, G)]
+        before = None
+        for k in range(G + 1):
+            now = {}
+            for n in range(k, G + 1):
+                if k == 0:
+                    value = (1.0 - rate[0]) * now[n - 1] if n else jnp.ones((ROWS, LANES), F32)
+                else:
+                    value = rate[k - 1] * before[n - 1]
+                    if n > k:
+                        value += (1.0 - rate[k]) * now[n - 1]
+                now[n] = value
+                moved_by[q, k, n] = value
+            before = now
     each(NB, lambda k: arrive_b(k).wait_recv())
 
     for b in range(NB):
@@ -288,34 +354,53 @@
     surface = (landed[0:ROWS], landed[ROWS : 2 * ROWS])
     deep = (landed[2 * ROWS : 3 * ROWS], jnp.zeros((ROWS, LANES), F32))
 
-    def substep(t, carry):
+    def macro_step(e, carry):
         hill, channel = carry[0:2], carry[2:4]
-        partial, hill_next = [], []
+        hill_next, kept = [], []
         for q in range(2):
-            hill_out = state[4 + q] * hill[q]
-            outflow = state[6 + q] * channel[q]
-            partial.append(channel[q] - outflow + hill_out + deep[q])
-            hill_next.append(hill[q] - hill_out + surface[q])
-            for s, part in enumerate(split2(outflow)):
-                rows = slice((q * 2 + s) * 32, (q * 2 + s + 1) * 32)
-                for c in range(ROWS):
-                    cols = slice(c * LANES, (c + 1) * LANES)
-                    value = jnp.broadcast_to(part[c : c + 1, :], (32, LANES)).astype(BF16)
-                    lhs_step[rows, cols] = value * row_step[:, cols]
-        spread = nn_dot(lhs_step[...], lane_step[...])
-        sums = []
-        for q in range(2):
-            both = spread[q * 64 : q * 64 + 32] + spread[q * 64 + 32 : q * 64 + 64]
-            send_ring[t, q] = both[ROWS:]
-            sums.append(both[:ROWS])
-        copy = ring(t)
-        copy.start()
-        transit_chunk(t + 4)
-        copy.wait_recv()
-        new = [partial[q] + sums[q] + recv_ring[t, q] for q in range(2)]
+            water_now = hill[q]
+            given = []
+            for _ in range(G):
+                hill_out = state[4 + q] * water_now
+                given.append(hill_out + deep[q])
+                water_now = water_now - hill_out + surface[q]
+            hill_next.append(water_now)
+            for k in range(G + 1):
+                total = moved_by[q, k, G] * channel[q]
+                for n in range(k, G):
+                    total += moved_by[q, k, n] * given[G - 1 - n]
+                if k == 0:
+                    kept.append(total)
+                    continue
+                for s, part in enumerate(split2(total)):
+                    start = 4 * OFF[k - 1] + (q * 2 + s) * (k + 1) * ROWS
+                    for c in range(ROWS):
+                        cols = slice(c * LANES, (c + 1) * LANES)
+                        value = jnp.broadcast_to(part[c : c + 1, :], (ROWS, LANES)).astype(BF16)
+                        value = jnp.concatenate([value] * (k + 1), axis=0)
+                        lhs_step[start : start + (k + 1) * ROWS, cols] = value * row_step[OFF[k - 1] : OFF[k], cols]
+        sums = [[0.0] * (G + 1) for _ in range(2)]
+        for k in range(G, 0, -1):
+            spread = nn_dot(lhs_step[4 * OFF[k - 1] : 4 * OFF[k], :], lane_step[k - 1])
+            count = (k + 1) * ROWS
+            for q in range(2):
+                both = spread[2 * q * count : (2 * q + 1) * count] + spread[(2 * q + 1) * count : (2 * q + 2) * count]
+                for m in range(k + 1):
+                    sums[q][m] = sums[q][m] + both[m * ROWS : (m + 1) * ROWS]
+        for m in range(G, 0, -1):
+            for q in range(2):
+                send_ring[e, m - 1, q] = sums[q][m]
+            ring(e, m).start()
+        for j in range(CHUNKS_STEP):
+            transit_chunk(e * CHUNKS_STEP + j)
+        new = [kept[q] + sums[q][0] for q in range(2)]
+        for m in range(1, G + 1):
+            ring(e, m).wait_recv()
+            for q in range(2):
+                new[q] = new[q] + recv_ring[e, m - 1, q]
         return (*hill_next, *new)
 
-    final = lax.fori_loop(0, NSUB, substep, tuple(state[q] for q in range(4)))
+    final = lax.fori_loop(0, STEPS, macro_step, tuple(state[q] for q in range(4)))
     stored = final[2] + final[3]
     inundation = stored / (stored + cap[...])
     lhs = jnp.concatenate(split3(inundation), axis=0).astype(BF16)
@@ -330,6 +415,8 @@
         cols = slice(c * LANES, (c + 1) * LANES)
         for q in range(4):
             river_out[q : q + 1, cols] = final[q][c : c + 1, :]
+    for j in range(CHUNKS_STEP * STEPS, BINS // CHUNK):
+        transit_chunk(j)
     stores = (
         pltpu.make_async_copy(tr_out, tr_hbm, out_sem.at[0]),
         pltpu.make_async_copy(river_out, river_hbm, out_sem.at[1]),
@@ -364,11 +451,11 @@
     each(NB, lambda k: copy_rb(k).wait_send())
     each(NA, lambda k: copy_ra(k).wait_send())
 
-    def ring_done(t, _):
-        ring(t).wait_send()
-        return 0
-
-    lax.fori_loop(0, NSUB, ring_done, 0)
+    for m in range(1, G):
+        upstream(m).wait_send()
+    for e in range(STEPS):
+        for m in range(1, G + 1):
+            ring(e, m).wait_send()
     for copy in (*stores, store):
         copy.wait()
 
@@ -451,12 +538,18 @@
             pltpu.VMEM((LANES, 1024), BF16),
             pltpu.VMEM((LANES, 1024), BF16),
             pltpu.VMEM((ROWS, 1024), F32),
-            pltpu.VMEM((ROWS * LANES, LANES), BF16),
-            pltpu.VMEM((32, ROWS * LANES), BF16),
-            pltpu.VMEM((128, ROWS * LANES), BF16),
+            pltpu.VMEM((G, ROWS * LANES, LANES), BF16),
+            pltpu.VMEM((OFF[G], ROWS * LANES), BF16),
+            pltpu.VMEM((4 * OFF[G], ROWS * LANES), BF16),
             pltpu.VMEM((9 * ROWS, 1024), BF16),
             pltpu.VMEM((16, 1024), BF16),
             pltpu.VMEM((8, ROWS, LANES), F32),
+            pltpu.VMEM((2, G + 1, G + 1, ROWS, LANES), F32),
+            pltpu.VMEM((G, 3, ROWS, LANES), F32),
+            pltpu.VMEM((3, ROWS, LANES), F32),
+            pltpu.VMEM((G + 1, ROWS, LANES), jnp.int32),
+            pltpu.VMEM((G, 2, ROWS, LANES), F32),
+            dma((G,)), dma((G,)),
             pltpu.VMEM((8, *tile), F32),
             pltpu.VMEM((NA, *tile), F32),
             pltpu.VMEM((NB, *tile), F32),
@@ -465,10 +558,10 @@
             pltpu.VMEM((NB, *tile), F32),
             pltpu.VMEM(tile, F32),
             pltpu.VMEM((NA, *tile), F32),
-            pltpu.VMEM((NSUB, 2, ROWS, LANES), F32),
-            pltpu.VMEM((NSUB, 2, ROWS, LANES), F32),
+            pltpu.VMEM((STEPS, G, 2, ROWS, LANES), F32),
+            pltpu.VMEM((STEPS, G, 2, ROWS, LANES), F32),
             dma((NA,)), dma((NA,)), dma((NB,)), dma((NB,)), dma((NB,)), dma((NB,)), dma((NA,)), dma((NA,)),
-            dma((NSUB,)), dma((NSUB,)),
+            dma((STEPS, G)), dma((STEPS, G)),
         ],
         compiler_params=pltpu.CompilerParams(
             collective_id=0, has_side_effects=True, vmem_limit_bytes=60 * 1024 * 1024),

time: 55.8 us -> 49.4 us (0.89)
  Pallas kernels: 55 us -> 48.5 us
    pallas_call x1, Pallas kernels: 52.7 us -> 46.2 us  [shards(): pl.pallas_call(main_kernel, out_shape=(jax.ShapeDtypeStruct((n_rows, LANE...]
where the time goes in v3:
time: 49.4 us; the launch traced here: 49.1 us
  Pallas kernels  48.5 us (98%)
  between operations  0.64 us (1%)
    pallas_call x1, Pallas kernels, shards(): pl.pallas_call(main_kernel, out_shape=(jax.ShapeDtypeStruct((n_rows, LANE...  46.2 us
    pallas_call x1, Pallas kernels, shards(): pl.pallas_call(survive_kernel, out_shape=(jax.ShapeDtypeStruct((n_rows, L...  2.27 us

profile of v3, /device:TPU:1, one launch (start us, length us, event | category | flops | bytes accessed | tf_op | source)
XLA Modules:
  0.0 49.1 jit_solution(6040206320521987686)
XLA Ops:
  0.6 46.2 %hour.1 = (f32[3072,128]{1,0:T(8,128)}, f32[1,128]{1,0:T(1,128)}, f32[4,2048]{1,0:T(4,128)}) custom-call(f32[48,64,128]{2,1,0:T(8,128)} %bio_in.1, f32[48,128]{1,0:T(8,128)} %area_in.1, f32[4,64]{1,0:T(4,128)} %traits_in.3, f32[5,128]{1,0:T(8,128)} %forcing_in.1, f32[4,128]{1,0:T(4,128)} %weight_in.1, f32[4,48,48]{2,1,0:T(8,128)} %trans_in.1, ...), custom_call_target="tpu_custom_call" | custom-call | tf_op jit(solution)/shard_map/hour/pallas_call | solution.py:506
  46.9 2.3 %survive.1 = (f32[3072,128]{1,0:T(8,128)}, f32[1,128]{1,0:T(1,128)}, f32[4,2048]{1,0:T(4,128)}) custom-call(f32[3072,128]{1,0:T(8,128)} %get-tuple-element.9.mass_in, f32[4,64]{1,0:T(4,128)} %traits_in.3, f32[1,128]{1,0:T(1,128)} %get-tuple-element.10.flooded_in, f32[4,2048]{1,0:T(4,128)} %get-tuple-element.11.river_in), custom_call_target="tpu_custom_call" | custom-call | tf_op jit(solution)/shard_map/survive/pallas_call | solution.py:574

commit v4 on v3

--- a/solution.py
+++ b/solution.py
@@ -18,11 +18,26 @@
 NB = 8
 ROWS = 16
 CHUNK = 4
-G = 4
+G = 6
 STEPS = NSUB // G
 CHUNKS_STEP = 12 // STEPS
+UNROLL = True
+EARLY = False
 A_PATHS = 3
-OFF = [ROWS * sum(j + 1 for j in range(1, k)) for k in range(1, G + 2)]
+WIDE = 2 * LANES
+PAD = [0] + [(k + 2) // 2 * 16 for k in range(1, G + 1)]
+OFF = [sum(PAD[: k + 1]) for k in range(G + 1)]
+
+
+def far_first(axes):
+    offsets = [()]
+    for size in axes:
+        offsets = [(*o, d) for o in offsets for d in range(size)]
+    return sorted(offsets, key=lambda o: -sum(min(d, n - d) if n > 2 else 0.3 * d for d, n in zip(o, axes)))[:-1]
+
+
+FAR_A = far_first((4, 4))
+FAR_B = far_first((4, 2))
 
 
 def split2(x):
@@ -51,7 +66,7 @@
     tr_out, flood_out, river_out, out_sem,
     bio, area, traits, forcing, weight, trans, src, share, tgt, step, water, rates, cap, in_sem, bio_sem,
     grown, tmat, rhs, onehot_src, lane_rcv, row_rcv, lane_step, row_step, lhs_step, lhs_rcv, lhs_back, state,
-    moved_by, table, table_send, path, path_rate, st_s, st_r,
+    fold, moved_by, table, table_send, path, path_rate, st_s, st_r,
     send_a, recv_a, send_b, recv_b, send_rb, recv_rb, send_ra, recv_ra, send_ring, recv_ring,
     sa_s, sa_r, sb_s, sb_r, rb_s, rb_r, ra_s, ra_r, ring_s, ring_r,
 ):
@@ -145,50 +160,58 @@
     for r in range(8):
         send_a[r] = picked[:, r * LANES : (r + 1) * LANES] * share[r : r + 1, :]
 
+    def at_a(k):
+        dx, dy = FAR_A[k - 1]
+        return (my_x + dx) % 4 * 4 + (my_y + dy) % 4
+
+    def at_b(k):
+        dz, dc = FAR_B[k - 1]
+        return (my_b // 2 + dz) % 4 * 2 + (my_b + dc) % 2
+
     def copy_a(k):
-        other = (my_a + k) % NA
+        other = at_a(k)
         return pltpu.make_async_remote_copy(
             src_ref=send_a.at[other // 2], dst_ref=recv_a.at[my_a], send_sem=sa_s.at[k], recv_sem=sa_r.at[my_a],
             device_id=peer_a(other), device_id_type=MESH)
 
     def arrive_a(k):
-        other = (my_a + k) % NA
+        other = at_a(k)
         return pltpu.make_async_remote_copy(
             src_ref=send_a.at[0], dst_ref=recv_a.at[other], send_sem=sa_s.at[k], recv_sem=sa_r.at[other],
             device_id=peer_a(other), device_id_type=MESH)
 
     def copy_b(k):
-        other = (my_b + k) % NB
+        other = at_b(k)
         return pltpu.make_async_remote_copy(
             src_ref=send_b.at[other], dst_ref=recv_b.at[my_b], send_sem=sb_s.at[k], recv_sem=sb_r.at[my_b],
             device_id=peer_b(other), device_id_type=MESH)
 
     def arrive_b(k):
-        other = (my_b + k) % NB
+        other = at_b(k)
         return pltpu.make_async_remote_copy(
             src_ref=send_b.at[other], dst_ref=recv_b.at[other], send_sem=sb_s.at[k], recv_sem=sb_r.at[other],
             device_id=peer_b(other), device_id_type=MESH)
 
     def copy_rb(k):
-        other = (my_b + k) % NB
+        other = at_b(k)
         return pltpu.make_async_remote_copy(
             src_ref=send_rb.at[other], dst_ref=recv_rb.at[my_b], send_sem=rb_s.at[k], recv_sem=rb_r.at[my_b],
             device_id=peer_b(other), device_id_type=MESH)
 
     def arrive_rb(k):
-        other = (my_b + k) % NB
+        other = at_b(k)
         return pltpu.make_async_remote_copy(
             src_ref=send_rb.at[other], dst_ref=recv_rb.at[other], send_sem=rb_s.at[k], recv_sem=rb_r.at[other],
             device_id=peer_b(other), device_id_type=MESH)
 
     def copy_ra(k):
-        other = (my_a + k) % NA
+        other = at_a(k)
         return pltpu.make_async_remote_copy(
             src_ref=send_ra, dst_ref=recv_ra.at[my_a], send_sem=ra_s.at[k], recv_sem=ra_r.at[my_a],
             device_id=peer_a(other), device_id_type=MESH)
 
     def arrive_ra(k):
-        other = (my_a + k) % NA
+        other = at_a(k)
         return pltpu.make_async_remote_copy(
             src_ref=send_ra, dst_ref=recv_ra.at[other], send_sem=ra_s.at[k], recv_sem=ra_r.at[other],
             device_id=peer_a(other), device_id_type=MESH)
@@ -207,11 +230,8 @@
             device_id=(to // 32, to % 32), device_id_type=MESH)
 
     def each(count, action):
-        def one(k, _):
+        for k in range(1, count):
             action(k)
-            return 0
-
-        lax.fori_loop(1, count, one, 0)
 
     pl.semaphore_wait(barrier, NA + NB - 2 + 2 * G)
     each(NA, lambda k: copy_a(k).start())
@@ -220,9 +240,11 @@
     loads[10].wait()
     for c in range(ROWS):
         cols = slice(c * LANES, (c + 1) * LANES)
+        wide = slice(c % 2 * LANES, (c % 2 + 1) * LANES)
         for q in range(2):
-            table_send[q, c : c + 1, :] = rates[2 + q : 3 + q, cols]
-    table_send[2] = step[...].astype(F32)
+            table_send[q, c // 2 : c // 2 + 1, wide] = rates[2 + q : 3 + q, cols]
+    for p in range(2):
+        table_send[2, :, p * LANES : (p + 1) * LANES] = step[pl.ds(p, 8, stride=2), :].astype(F32)
     for m in range(1, G):
         upstream(m).start()
     table[0] = table_send[...]
@@ -255,9 +277,11 @@
     stride = step[...]
     path[1] = jnp.where(stride > 0, sub16 * LANES + lane16 + stride, -1)
 
+    sub256 = lax.broadcasted_iota(jnp.int32, (WIDE, LANES), 0)
+
     def follow(k):
-        count = (k + 1) * ROWS
-        sub_rows = lax.broadcasted_iota(jnp.int32, (count, LANES), 0)
+        count = (k + 1) * 8
+        sub_rows = lax.broadcasted_iota(jnp.int32, (PAD[k], LANES), 0)
         if k < G:
             fields = []
             for f in range(3):
@@ -270,23 +294,23 @@
                 c = i * 4 + j
                 cells = path[k, pl.ds(c, 1), :]
                 cols = pl.ds(pl.multiple_of(c * LANES, LANES), LANES)
-                hot = jnp.where(sub128 == (cells & (LANES - 1)), 1.0, 0.0)
-                lane_step[k - 1, cols, :] = hot.T.astype(BF16)
-                rows = jnp.where(sub_rows == (cells >> 7), 1.0, 0.0)
-                row_step[OFF[k - 1] : OFF[k - 1] + count, cols] = rows.astype(BF16)
+                hot = jnp.where(sub256 == (cells & (WIDE - 1)), 1.0, 0.0).astype(BF16)
+                lane_step[k - 1, :, cols] = hot
+                rows = jnp.where(sub_rows == (cells >> 8), 1.0, 0.0)
+                row_step[OFF[k - 1] : OFF[k], cols] = rows.astype(BF16)
                 if k < G:
-                    found = nn_dot(lookup, hot.astype(BF16))
+                    found = nn_dot(lookup, hot)
                     values = []
                     for f in range(3):
                         both = found[2 * f * count : (2 * f + 1) * count] + found[(2 * f + 1) * count : (2 * f + 2) * count]
-                        values.append(jnp.sum(both * rows, axis=0, keepdims=True))
+                        values.append(jnp.sum(both * rows[:count], axis=0, keepdims=True))
                     path_rate[k, 0, pl.ds(c, 1), :] = values[0]
                     path_rate[k, 1, pl.ds(c, 1), :] = values[1]
                     hop = (values[2] + 0.5).astype(jnp.int32)
                     path[k + 1, pl.ds(c, 1), :] = jnp.where(hop > 0, cells + hop, -1)
             return 0
 
-        lax.fori_loop(0, 4, piece, 0)
+        lax.fori_loop(0, 4, piece, 0, unroll=UNROLL)
 
     listed = jnp.zeros((8, LANES), jnp.int32)
     for a in range(NA):
@@ -327,7 +351,7 @@
     for k in range(A_PATHS, G + 1):
         follow(k)
     for q in range(2):
-        rate = [table[0, q]] + [path_rate[k, q] for k in range(1, G)]
+        rate = [state[6 + q]] + [path_rate[k, q] for k in range(1, G)]
         before = None
         for k in range(G + 1):
             now = {}
@@ -356,7 +380,7 @@
 
     def macro_step(e, carry):
         hill, channel = carry[0:2], carry[2:4]
-        hill_next, kept = [], []
+        hill_next, kept, masses = [], [], [{}, {}]
         for q in range(2):
             water_now = hill[q]
             given = []
@@ -372,32 +396,45 @@
                 if k == 0:
                     kept.append(total)
                     continue
-                for s, part in enumerate(split2(total)):
-                    start = 4 * OFF[k - 1] + (q * 2 + s) * (k + 1) * ROWS
-                    for c in range(ROWS):
-                        cols = slice(c * LANES, (c + 1) * LANES)
-                        value = jnp.broadcast_to(part[c : c + 1, :], (ROWS, LANES)).astype(BF16)
-                        value = jnp.concatenate([value] * (k + 1), axis=0)
-                        lhs_step[start : start + (k + 1) * ROWS, cols] = value * row_step[OFF[k - 1] : OFF[k], cols]
+                masses[q][k] = total
         sums = [[0.0] * (G + 1) for _ in range(2)]
-        for k in range(G, 0, -1):
-            spread = nn_dot(lhs_step[4 * OFF[k - 1] : 4 * OFF[k], :], lane_step[k - 1])
-            count = (k + 1) * ROWS
-            for q in range(2):
-                both = spread[2 * q * count : (2 * q + 1) * count] + spread[(2 * q + 1) * count : (2 * q + 2) * count]
-                for m in range(k + 1):
-                    sums[q][m] = sums[q][m] + both[m * ROWS : (m + 1) * ROWS]
-        for m in range(G, 0, -1):
+
+        def send(m):
             for q in range(2):
                 send_ring[e, m - 1, q] = sums[q][m]
             ring(e, m).start()
+
+        for k in range(G, 0, -1):
+            pad = PAD[k]
+            for q in range(2):
+                for s, part in enumerate(split2(masses[q][k])):
+                    start = 4 * OFF[k - 1] + (q * 2 + s) * pad
+                    for c in range(ROWS):
+                        cols = slice(c * LANES, (c + 1) * LANES)
+                        value = jnp.broadcast_to(part[c : c + 1, :], (16, LANES)).astype(BF16)
+                        value = jnp.concatenate([value] * (pad // 16), axis=0)
+                        lhs_step[start : start + pad, cols] = value * row_step[OFF[k - 1] : OFF[k], cols]
+            spread = nt_dot(lhs_step[4 * OFF[k - 1] : 4 * OFF[k], :], lane_step[k - 1])
+            for q in range(2):
+                both = spread[2 * q * pad : (2 * q + 1) * pad] + spread[(2 * q + 1) * pad : (2 * q + 2) * pad]
+                for m in range(k + 1):
+                    sums[q][m] = sums[q][m] + both[m * 8 : (m + 1) * 8]
+            if EARLY:
+                send(k)
+        if not EARLY:
+            for m in range(G, 0, -1):
+                send(m)
         for j in range(CHUNKS_STEP):
             transit_chunk(e * CHUNKS_STEP + j)
-        new = [kept[q] + sums[q][0] for q in range(2)]
+        came = [sums[q][0] for q in range(2)]
         for m in range(1, G + 1):
             ring(e, m).wait_recv()
             for q in range(2):
-                new[q] = new[q] + recv_ring[e, m - 1, q]
+                came[q] = came[q] + recv_ring[e, m - 1, q]
+        for q in range(2):
+            fold[q, pl.ds(0, 8, stride=2), :] = came[q][:, :LANES]
+            fold[q, pl.ds(1, 8, stride=2), :] = came[q][:, LANES:]
+        new = [kept[q] + fold[q] for q in range(2)]
         return (*hill_next, *new)
 
     final = lax.fori_loop(0, STEPS, macro_step, tuple(state[q] for q in range(4)))
@@ -538,15 +575,16 @@
             pltpu.VMEM((LANES, 1024), BF16),
             pltpu.VMEM((LANES, 1024), BF16),
             pltpu.VMEM((ROWS, 1024), F32),
-            pltpu.VMEM((G, ROWS * LANES, LANES), BF16),
+            pltpu.VMEM((G, WIDE, ROWS * LANES), BF16),
             pltpu.VMEM((OFF[G], ROWS * LANES), BF16),
             pltpu.VMEM((4 * OFF[G], ROWS * LANES), BF16),
             pltpu.VMEM((9 * ROWS, 1024), BF16),
             pltpu.VMEM((16, 1024), BF16),
             pltpu.VMEM((8, ROWS, LANES), F32),
+            pltpu.VMEM((2, ROWS, LANES), F32),
             pltpu.VMEM((2, G + 1, G + 1, ROWS, LANES), F32),
-            pltpu.VMEM((G, 3, ROWS, LANES), F32),
-            pltpu.VMEM((3, ROWS, LANES), F32),
+            pltpu.VMEM((G, 3, 8, WIDE), F32),
+            pltpu.VMEM((3, 8, WIDE), F32),
             pltpu.VMEM((G + 1, ROWS, LANES), jnp.int32),
             pltpu.VMEM((G, 2, ROWS, LANES), F32),
             dma((G,)), dma((G,)),
@@ -558,8 +596,8 @@
             pltpu.VMEM((NB, *tile), F32),
             pltpu.VMEM(tile, F32),
             pltpu.VMEM((NA, *tile), F32),
-            pltpu.VMEM((STEPS, G, 2, ROWS, LANES), F32),
-            pltpu.VMEM((STEPS, G, 2, ROWS, LANES), F32),
+            pltpu.VMEM((STEPS, G, 2, 8, WIDE), F32),
+            pltpu.VMEM((STEPS, G, 2, 8, WIDE), F32),
             dma((NA,)), dma((NA,)), dma((NB,)), dma((NB,)), dma((NB,)), dma((NB,)), dma((NA,)), dma((NA,)),
             dma((STEPS, G)), dma((STEPS, G)),
         ],

time: 49.4 us -> 46.2 us (0.935)
  Pallas kernels: 48.5 us -> 45.4 us
    pallas_call x1, Pallas kernels: 46.2 us -> 43.1 us  [shards(): pl.pallas_call(main_kernel, out_shape=(jax.ShapeDtypeStruct((n_rows, LANE...]
where the time goes in v4:
time: 46.2 us; the launch traced here: 46 us
  Pallas kernels  45.4 us (98%)
  between operations  0.64 us (1%)
    pallas_call x1, Pallas kernels, shards(): pl.pallas_call(main_kernel, out_shape=(jax.ShapeDtypeStruct((n_rows, LANE...  43.1 us
    pallas_call x1, Pallas kernels, shards(): pl.pallas_call(survive_kernel, out_shape=(jax.ShapeDtypeStruct((n_rows, L...  2.27 us

profile of v4, /device:TPU:1, one launch (start us, length us, event | category | flops | bytes accessed | tf_op | source)
XLA Modules:
  0.0 46.0 jit_solution(7304827733936559802)
XLA Ops:
  0.6 43.1 %hour.1 = (f32[3072,128]{1,0:T(8,128)}, f32[1,128]{1,0:T(1,128)}, f32[4,2048]{1,0:T(4,128)}) custom-call(f32[48,64,128]{2,1,0:T(8,128)} %bio_in.1, f32[48,128]{1,0:T(8,128)} %area_in.1, f32[4,64]{1,0:T(4,128)} %traits_in.3, f32[5,128]{1,0:T(8,128)} %forcing_in.1, f32[4,128]{1,0:T(4,128)} %weight_in.1, f32[4,48,48]{2,1,0:T(8,128)} %trans_in.1, ...), custom_call_target="tpu_custom_call" | custom-call | tf_op jit(solution)/shard_map/hour/pallas_call | solution.py:543
  43.8 2.3 %survive.1 = (f32[3072,128]{1,0:T(8,128)}, f32[1,128]{1,0:T(1,128)}, f32[4,2048]{1,0:T(4,128)}) custom-call(f32[3072,128]{1,0:T(8,128)} %get-tuple-element.9.mass_in, f32[4,64]{1,0:T(4,128)} %traits_in.3, f32[1,128]{1,0:T(1,128)} %get-tuple-element.10.flooded_in, f32[4,2048]{1,0:T(4,128)} %get-tuple-element.11.river_in), custom_call_target="tpu_custom_call" | custom-call | tf_op jit(solution)/shard_map/survive/pallas_call | solution.py:612

commit v5 on v4

--- a/solution.py
+++ b/solution.py
@@ -277,7 +277,7 @@
     stride = step[...]
     path[1] = jnp.where(stride > 0, sub16 * LANES + lane16 + stride, -1)
 
-    sub256 = lax.broadcasted_iota(jnp.int32, (WIDE, LANES), 0)
+    sub256 = lax.broadcasted_iota(jnp.int32, (WIDE, LANES), 0).astype(F32).astype(BF16)
 
     def follow(k):
         count = (k + 1) * 8
@@ -294,8 +294,10 @@
                 c = i * 4 + j
                 cells = path[k, pl.ds(c, 1), :]
                 cols = pl.ds(pl.multiple_of(c * LANES, LANES), LANES)
-                hot = jnp.where(sub256 == (cells & (WIDE - 1)), 1.0, 0.0).astype(BF16)
-                lane_step[k - 1, :, cols] = hot
+                lane = jnp.broadcast_to((cells & (WIDE - 1)).astype(F32), (16, LANES)).astype(BF16)
+                lane = jnp.concatenate([lane] * (WIDE // 16), axis=0)
+                hot = jnp.where(sub256 == lane, jnp.ones_like(lane), jnp.zeros_like(lane))
+                lane_step[k - 1, cols, :] = hot.T
                 rows = jnp.where(sub_rows == (cells >> 8), 1.0, 0.0)
                 row_step[OFF[k - 1] : OFF[k], cols] = rows.astype(BF16)
                 if k < G:
@@ -414,7 +416,7 @@
                         value = jnp.broadcast_to(part[c : c + 1, :], (16, LANES)).astype(BF16)
                         value = jnp.concatenate([value] * (pad // 16), axis=0)
                         lhs_step[start : start + pad, cols] = value * row_step[OFF[k - 1] : OFF[k], cols]
-            spread = nt_dot(lhs_step[4 * OFF[k - 1] : 4 * OFF[k], :], lane_step[k - 1])
+            spread = nn_dot(lhs_step[4 * OFF[k - 1] : 4 * OFF[k], :], lane_step[k - 1])
             for q in range(2):
                 both = spread[2 * q * pad : (2 * q + 1) * pad] + spread[(2 * q + 1) * pad : (2 * q + 2) * pad]
                 for m in range(k + 1):
@@ -575,7 +577,7 @@
             pltpu.VMEM((LANES, 1024), BF16),
             pltpu.VMEM((LANES, 1024), BF16),
             pltpu.VMEM((ROWS, 1024), F32),
-            pltpu.VMEM((G, WIDE, ROWS * LANES), BF16),
+            pltpu.VMEM((G, ROWS * LANES, WIDE), BF16),
             pltpu.VMEM((OFF[G], ROWS * LANES), BF16),
             pltpu.VMEM((4 * OFF[G], ROWS * LANES), BF16),
             pltpu.VMEM((9 * ROWS, 1024), BF16),

time: 46.2 us -> 44.9 us (0.972)
  Pallas kernels: 45.4 us -> 44.1 us
    pallas_call x1, Pallas kernels: 43.1 us -> 41.8 us  [shards(): pl.pallas_call(main_kernel, out_shape=(jax.ShapeDtypeStruct((n_rows, LANE...]
where the time goes in v5:
time: 44.9 us; the launch traced here: 44.7 us
  Pallas kernels  44.1 us (98%)
  between operations  0.64 us (1%)
    pallas_call x1, Pallas kernels, shards(): pl.pallas_call(main_kernel, out_shape=(jax.ShapeDtypeStruct((n_rows, LANE...  41.8 us
    pallas_call x1, Pallas kernels, shards(): pl.pallas_call(survive_kernel, out_shape=(jax.ShapeDtypeStruct((n_rows, L...  2.27 us

profile of v5, /device:TPU:1, one launch (start us, length us, event | category | flops | bytes accessed | tf_op | source)
XLA Modules:
  0.0 44.7 jit_solution(15248407637426161684)
XLA Ops:
  0.6 41.8 %hour.1 = (f32[3072,128]{1,0:T(8,128)}, f32[1,128]{1,0:T(1,128)}, f32[4,2048]{1,0:T(4,128)}) custom-call(f32[48,64,128]{2,1,0:T(8,128)} %bio_in.1, f32[48,128]{1,0:T(8,128)} %area_in.1, f32[4,64]{1,0:T(4,128)} %traits_in.3, f32[5,128]{1,0:T(8,128)} %forcing_in.1, f32[4,128]{1,0:T(4,128)} %weight_in.1, f32[4,48,48]{2,1,0:T(8,128)} %trans_in.1, ...), custom_call_target="tpu_custom_call" | custom-call | tf_op jit(solution)/shard_map/hour/pallas_call | solution.py:545
  42.5 2.3 %survive.1 = (f32[3072,128]{1,0:T(8,128)}, f32[1,128]{1,0:T(1,128)}, f32[4,2048]{1,0:T(4,128)}) custom-call(f32[3072,128]{1,0:T(8,128)} %get-tuple-element.9.mass_in, f32[4,64]{1,0:T(4,128)} %traits_in.3, f32[1,128]{1,0:T(1,128)} %get-tuple-element.10.flooded_in, f32[4,2048]{1,0:T(4,128)} %get-tuple-element.11.river_in), custom_call_target="tpu_custom_call" | custom-call | tf_op jit(solution)/shard_map/survive/pallas_call | solution.py:614

commit v6 on v5

--- a/solution.py
+++ b/solution.py
@@ -22,7 +22,7 @@
 STEPS = NSUB // G
 CHUNKS_STEP = 12 // STEPS
 UNROLL = True
-EARLY = False
+EARLY = 3
 A_PATHS = 3
 WIDE = 2 * LANES
 PAD = [0] + [(k + 2) // 2 * 16 for k in range(1, G + 1)]
@@ -49,10 +49,6 @@
     hi, rest = split2(x)
     mid, low = split2(rest)
     return hi, mid, low
-
-
-def nt_dot(a, b):
-    return lax.dot_general(a, b, (((1,), (1,)), ((), ())), preferred_element_type=F32)
 
 
 def nn_dot(a, b):
@@ -65,11 +61,35 @@
     tr_hbm, flood_hbm, river_hbm,
     tr_out, flood_out, river_out, out_sem,
     bio, area, traits, forcing, weight, trans, src, share, tgt, step, water, rates, cap, in_sem, bio_sem,
-    grown, tmat, rhs, onehot_src, lane_rcv, row_rcv, lane_step, row_step, lhs_step, lhs_rcv, lhs_back, state,
+    grown, tmat, rhs, onehot_src, lane_rcv_t, onehot_src_t, lane_rcv, row_rcv, lane_step, row_step, lhs_step, lhs_rcv, lhs_back, state,
     fold, moved_by, table, table_send, path, path_rate, st_s, st_r,
     send_a, recv_a, send_b, recv_b, send_rb, recv_rb, send_ra, recv_ra, send_ring, recv_ring,
     sa_s, sa_r, sb_s, sb_r, rb_s, rb_r, ra_s, ra_r, ring_s, ring_r,
 ):
+    my_x = lax.axis_index("comp")
+    cell = lax.axis_index("cell")
+    my_y, my_b = cell // NB, cell % NB
+    my_a = my_x * 4 + my_y
+    me = my_x * 32 + cell
+
+    def peer_a(other):
+        return (other // 4, (other % 4) * NB + my_b)
+
+    def peer_b(other):
+        return (my_x, my_y * NB + other)
+
+    barrier = pltpu.get_barrier_semaphore()
+
+    for dx, dy in FAR_A:
+        peer = peer_a((my_x + dx) % 4 * 4 + (my_y + dy) % 4)
+        pl.semaphore_signal(barrier, inc=1, device_id=peer, device_id_type=MESH)
+    for dz, dc in FAR_B:
+        peer = peer_b((my_b // 2 + dz) % 4 * 2 + (my_b + dc) % 2)
+        pl.semaphore_signal(barrier, inc=1, device_id=peer, device_id_type=MESH)
+    for m in range(1, G + 1):
+        for other in ((me + m) % 128, (me + 128 - m) % 128):
+            pl.semaphore_signal(barrier, inc=1, device_id=(other // 32, other % 32), device_id_type=MESH)
+
     sources = (area_in, traits_in, forcing_in, weight_in, trans_in, src_in, share_in, tgt_in, step_in, water_in, rates_in, cap_in)
     targets = (area, traits, forcing, weight, trans, src, share, tgt, step, water, rates, cap)
     loads = [pltpu.make_async_copy(sources[i], targets[i], in_sem.at[i]) for i in range(12)]
@@ -82,34 +102,6 @@
         mass_loads[g].start()
     for i in (0, 6, 4, 3, 8, 7, 9, 10, 11):
         loads[i].start()
-    my_x = lax.axis_index("comp")
-    cell = lax.axis_index("cell")
-    my_y, my_b = cell // NB, cell % NB
-    my_a = my_x * 4 + my_y
-    me = my_x * 32 + cell
-
-    def peer_a(other):
-        return (other // 4, (other % 4) * NB + my_b)
-
-    def peer_b(other):
-        return (my_x, my_y * NB + other)
-
-    barrier = pltpu.get_barrier_semaphore()
-
-    def greet_a(k, _):
-        pl.semaphore_signal(barrier, inc=1, device_id=peer_a((my_a + k) % NA), device_id_type=MESH)
-        return 0
-
-    def greet_b(k, _):
-        pl.semaphore_signal(barrier, inc=1, device_id=peer_b((my_b + k) % NB), device_id_type=MESH)
-        return 0
-
-    lax.fori_loop(1, NA, greet_a, 0)
-    lax.fori_loop(1, NB, greet_b, 0)
-    for m in range(1, G + 1):
-        for other in ((me + m) % 128, (me + 128 - m) % 128):
-            pl.semaphore_signal(barrier, inc=1, device_id=(other // 32, other % 32), device_id_type=MESH)
-
     sub8 = lax.broadcasted_iota(jnp.int32, (8, LANES), 0)
     lane8 = lax.broadcasted_iota(jnp.int32, (8, LANES), 1)
     block8 = lane8 >> 3
@@ -325,7 +317,9 @@
     list_row = listed >> 7
     for b in range(NB):
         cols = slice(b * LANES, (b + 1) * LANES)
-        lane_rcv[:, cols] = jnp.where(sub128 == list_lane[b : b + 1, :], 1.0, 0.0).astype(BF16)
+        hot = jnp.where(sub128 == list_lane[b : b + 1, :], 1.0, 0.0).astype(BF16)
+        lane_rcv[:, cols] = hot
+        lane_rcv_t[cols, :] = hot.T
         row_rcv[:, cols] = jnp.where(sub16 == list_row[b : b + 1, :], 1.0, 0.0)
 
     for c in range(ROWS):
@@ -333,9 +327,8 @@
         for q in range(4):
             state[q, c : c + 1, :] = water[q : q + 1, cols]
             state[4 + q, c : c + 1, :] = rates[q : q + 1, cols]
-    for m in range(1, G):
-        upstream(m).wait_recv()
     for k in range(1, A_PATHS):
+        upstream(k).wait_recv()
         follow(k)
 
     each(NA, lambda k: arrive_a(k).wait_recv())
@@ -351,6 +344,8 @@
     each(NB, lambda k: copy_b(k).start())
     recv_b[my_b] = send_b[my_b]
     for k in range(A_PATHS, G + 1):
+        if k < G:
+            upstream(k).wait_recv()
         follow(k)
     for q in range(2):
         rate = [state[6 + q]] + [path_rate[k, q] for k in range(1, G)]
@@ -375,7 +370,7 @@
         for s, part in enumerate(split3(recv_b[b])):
             for f in range(3):
                 lhs_rcv[(s * 3 + f) * ROWS : (s * 3 + f + 1) * ROWS, cols] = (part[f : f + 1, :] * hot).astype(BF16)
-    landed = nt_dot(lhs_rcv[...], lane_rcv[...])
+    landed = nn_dot(lhs_rcv[...], lane_rcv_t[...])
     landed = (landed[0:48] + landed[48:96] + landed[96:144]) * (1.0 / NSUB)
     surface = (landed[0:ROWS], landed[ROWS : 2 * ROWS])
     deep = (landed[2 * ROWS : 3 * ROWS], jnp.zeros((ROWS, LANES), F32))
@@ -421,11 +416,11 @@
                 both = spread[2 * q * pad : (2 * q + 1) * pad] + spread[(2 * q + 1) * pad : (2 * q + 2) * pad]
                 for m in range(k + 1):
                     sums[q][m] = sums[q][m] + both[m * 8 : (m + 1) * 8]
-            if EARLY:
-                send(k)
-        if not EARLY:
-            for m in range(G, 0, -1):
-                send(m)
+            if k == EARLY:
+                for m in range(G, EARLY - 1, -1):
+                    send(m)
+        for m in range(EARLY - 1, 0, -1):
+            send(m)
         for j in range(CHUNKS_STEP):
             transit_chunk(e * CHUNKS_STEP + j)
         came = [sums[q][0] for q in range(2)]
@@ -454,6 +449,9 @@
         cols = slice(c * LANES, (c + 1) * LANES)
         for q in range(4):
             river_out[q : q + 1, cols] = final[q][c : c + 1, :]
+    for r in range(8):
+        cols = slice(r * LANES, (r + 1) * LANES)
+        onehot_src_t[cols, :] = onehot_src[:, cols].T
     for j in range(CHUNKS_STEP * STEPS, BINS // CHUNK):
         transit_chunk(j)
     stores = (
@@ -480,7 +478,7 @@
         hi, mid, low = split3(row)
         tile = jnp.where(sub16 == 0, hi, jnp.where(sub16 == 1, mid, jnp.where(sub16 == 2, low, 0.0)))
         lhs_back[:, r * LANES : (r + 1) * LANES] = tile.astype(BF16)
-    felt = nt_dot(lhs_back[...], onehot_src[...])
+    felt = nn_dot(lhs_back[...], onehot_src_t[...])
     flood_out[...] = felt[0:1] + felt[1:2] + felt[2:3]
     store = pltpu.make_async_copy(flood_out, flood_hbm, out_sem.at[2])
     store.start()
@@ -575,6 +573,8 @@
             pltpu.VMEM((KINDS * PATCH, 3 * PATCH), BF16),
             pltpu.VMEM((3 * PATCH, CHUNK * LANES), BF16),
             pltpu.VMEM((LANES, 1024), BF16),
+            pltpu.VMEM((1024, LANES), BF16),
+            pltpu.VMEM((1024, LANES), BF16),
             pltpu.VMEM((LANES, 1024), BF16),
             pltpu.VMEM((ROWS, 1024), F32),
             pltpu.VMEM((G, ROWS * LANES, WIDE), BF16),

time: 44.9 us -> 43.3 us (0.964)
  Pallas kernels: 44.1 us -> 42.5 us
    pallas_call x1, Pallas kernels: 41.8 us -> 40.2 us  [shards(): pl.pallas_call(main_kernel, out_shape=(jax.ShapeDtypeStruct((n_rows, LANE...]
where the time goes in v6:
time: 43.3 us; the launch traced here: 43.1 us
  Pallas kernels  42.5 us (98%)
  between operations  0.64 us (1%)
    pallas_call x1, Pallas kernels, shards(): pl.pallas_call(main_kernel, out_shape=(jax.ShapeDtypeStruct((n_rows, LANE...  40.2 us
    pallas_call x1, Pallas kernels, shards(): pl.pallas_call(survive_kernel, out_shape=(jax.ShapeDtypeStruct((n_rows, L...  2.27 us

profile of v6, /device:TPU:1, one launch (start us, length us, event | category | flops | bytes accessed | tf_op | source)
XLA Modules:
  0.0 43.1 jit_solution(16071273171034554210)
XLA Ops:
  0.6 40.2 %hour.1 = (f32[3072,128]{1,0:T(8,128)}, f32[1,128]{1,0:T(1,128)}, f32[4,2048]{1,0:T(4,128)}) custom-call(f32[48,64,128]{2,1,0:T(8,128)} %bio_in.1, f32[48,128]{1,0:T(8,128)} %area_in.1, f32[4,64]{1,0:T(4,128)} %traits_in.3, f32[5,128]{1,0:T(8,128)} %forcing_in.1, f32[4,128]{1,0:T(4,128)} %weight_in.1, f32[4,48,48]{2,1,0:T(8,128)} %trans_in.1, ...), custom_call_target="tpu_custom_call" | custom-call | tf_op jit(solution)/shard_map/hour/pallas_call | solution.py:543
  40.9 2.3 %survive.1 = (f32[3072,128]{1,0:T(8,128)}, f32[1,128]{1,0:T(1,128)}, f32[4,2048]{1,0:T(4,128)}) custom-call(f32[3072,128]{1,0:T(8,128)} %get-tuple-element.9.mass_in, f32[4,64]{1,0:T(4,128)} %traits_in.3, f32[1,128]{1,0:T(1,128)} %get-tuple-element.10.flooded_in, f32[4,2048]{1,0:T(4,128)} %get-tuple-element.11.river_in), custom_call_target="tpu_custom_call" | custom-call | tf_op jit(solution)/shard_map/survive/pallas_call | solution.py:614

commit v7 on v6

--- a/solution.py
+++ b/solution.py
@@ -23,7 +23,7 @@
 CHUNKS_STEP = 12 // STEPS
 UNROLL = True
 EARLY = 3
-A_PATHS = 3
+A_PATHS = 2
 WIDE = 2 * LANES
 PAD = [0] + [(k + 2) // 2 * 16 for k in range(1, G + 1)]
 OFF = [sum(PAD[: k + 1]) for k in range(G + 1)]

time: 43.3 us -> 42.4 us (0.979)
  Pallas kernels: 42.5 us -> 41.3 us
    pallas_call x1, Pallas kernels: 40.2 us -> 39 us  [shards(): pl.pallas_call(main_kernel, out_shape=(jax.ShapeDtypeStruct((n_rows, LANE...]
where the time goes in v7:
time: 42.4 us; the launch traced here: 41.9 us
  Pallas kernels  41.3 us (97%)
  between operations  0.64 us (2%)
    pallas_call x1, Pallas kernels, shards(): pl.pallas_call(main_kernel, out_shape=(jax.ShapeDtypeStruct((n_rows, LANE...  39 us
    pallas_call x1, Pallas kernels, shards(): pl.pallas_call(survive_kernel, out_shape=(jax.ShapeDtypeStruct((n_rows, L...  2.27 us

profile of v7, /device:TPU:1, one launch (start us, length us, event | category | flops | bytes accessed | tf_op | source)
XLA Modules:
  0.0 41.9 jit_solution(3740427739651412159)
XLA Ops:
  0.6 39.0 %hour.1 = (f32[3072,128]{1,0:T(8,128)}, f32[1,128]{1,0:T(1,128)}, f32[4,2048]{1,0:T(4,128)}) custom-call(f32[48,64,128]{2,1,0:T(8,128)} %bio_in.1, f32[48,128]{1,0:T(8,128)} %area_in.1, f32[4,64]{1,0:T(4,128)} %traits_in.3, f32[5,128]{1,0:T(8,128)} %forcing_in.1, f32[4,128]{1,0:T(4,128)} %weight_in.1, f32[4,48,48]{2,1,0:T(8,128)} %trans_in.1, ...), custom_call_target="tpu_custom_call" | custom-call | tf_op jit(solution)/shard_map/hour/pallas_call | solution.py:543
  39.7 2.3 %survive.1 = (f32[3072,128]{1,0:T(8,128)}, f32[1,128]{1,0:T(1,128)}, f32[4,2048]{1,0:T(4,128)}) custom-call(f32[3072,128]{1,0:T(8,128)} %get-tuple-element.9.mass_in, f32[4,64]{1,0:T(4,128)} %traits_in.3, f32[1,128]{1,0:T(1,128)} %get-tuple-element.10.flooded_in, f32[4,2048]{1,0:T(4,128)} %get-tuple-element.11.river_in), custom_call_target="tpu_custom_call" | custom-call | tf_op jit(solution)/shard_map/survive/pallas_call | solution.py:614
